TPU v7x, 128 devices: a whole 4x4x4 slice. The times are simulated.
128 devices in a mesh: lat: 16 (over y_hi, x, core), lon: 8 (over y_lo, z).
Axes of the slice: x: 4, y: 4 (y_hi: 2, y_lo: 2; y = y_hi * 2 + y_lo), z: 4, core: 2. Of those that a mesh axis runs over, the one named last changes fastest.
Arguments:
- ensemble: float32 [2, 1, 2048, 16384], P(None, None, 'lat', 'lon'), may hold values from -6 to 6
- cross_mix: float32 [2, 2048, 16384], P(None, 'lat', 'lon'), may hold values from -0.5 to 0.5
- sea_mask: int32 [2048, 16384], P('lat', 'lon'), may hold values 0 or 1
- level_rates: float32 [2, 2], replicated, may hold values from 1 to 256, as said below
- panel_inverse: float32 [2, 2, 128, 128], replicated, may hold values from 0 to 1, as said below
- reduced_lon: float32 [2, 256, 256], replicated, as said below
- reduced_lat: float32 [2, 32, 32], replicated, as said below
Outputs:
- smoothed: float32 [2, 1, 2048, 16384], P(None, None, 'lat', 'lon')
Inputs may be any that keep to these rules, and one draw needn't show every extreme that they name: `level_rates`: the same for every point of a level. `panel_inverse`: the inverse of the 128 x 128 tridiagonal matrix whose diagonal entries are one plus twice a (that is 1 + 2*a) and whose entries beside the diagonal are -a, a taken from level_rates. `reduced_lon`: the inverse of the system that the longitude line solve's panel end values satisfy, for the given panel inverses and rates. `reduced_lat`: the inverse of the system that the latitude line solve's panel end values satisfy, for the given panel inverses and rates.
All inputs are finite; a program needn't handle non-finite values. No bound on the sum of `sea_mask` on one device may be relied on, other than what follows from the above.
Results may differ from a plain program's by a relative error of at most 0.00018.
Values sent between devices are 32-bit elements; how exact they have to be, the bound alone decides.
No kernel may reach another device: no remote copies, remote signals or barrier semaphores. Data moves between devices by JAX's collectives and lax.ppermute only.
A program may use at most 128 MiB of HBM per device.

v0:
```python
import jax
import jax.numpy as jnp
from jax import lax
from jax.sharding import PartitionSpec as P

STEPS = 2


highest = lax.Precision.HIGHEST


def with_halo(shard, sides, width, wrap):
    for axis, dim in sides:
        size, length = (lax.axis_size(axis), shard.shape[dim])
        up = [(i, (i + 1) % size) for i in range(size if wrap else size - 1)]
        down = [(j, i) for i, j in up]
        last = lax.slice_in_dim(shard, length - width, length, axis=dim)
        first = lax.slice_in_dim(shard, 0, width, axis=dim)
        before = lax.ppermute(last, axis, up)
        after = lax.ppermute(first, axis, down)
        shard = jnp.concatenate([before, shard, after], axis=dim)
    return shard


def cross_term(extended):
    return (
        extended[:, :, 2:, 2:]
        - extended[:, :, 2:, :-2]
        - extended[:, :, :-2, 2:]
        + extended[:, :, :-2, :-2]
    )


def explicit_terms(extended):
    centre = extended[:, :, 1:-1, 1:-1]
    along_lon = extended[:, :, 1:-1, 2:] - 2.0 * centre + extended[:, :, 1:-1, :-2]
    along_lat = extended[:, :, 2:, 1:-1] - 2.0 * centre + extended[:, :, :-2, 1:-1]
    return (along_lon, along_lat, cross_term(extended))


def lon_panels(values, inverse):
    panel = inverse.shape[1]
    dims = values.shape
    split = values.reshape(dims[:3] + (dims[3] // panel, panel))
    return jnp.einsum("lsrcq,lpq->lsrcp", split, inverse, precision=highest)


def lon_ends(solved):
    paired = jnp.stack((solved[..., 0], solved[..., -1]), axis=-1)
    return paired.reshape(paired.shape[:3] + (-1,))


def lon_finish(solved, prev_last, next_first, inverse, rate_lon):
    left_col = inverse[:, None, None, None, :, 0]
    right_col = inverse[:, None, None, None, :, -1]
    scale = rate_lon[:, None, None, None, None]
    result = solved + scale * (prev_last[..., None] * left_col + next_first[..., None] * right_col)
    return result.reshape(result.shape[:3] + (-1,))


def lon_solve(values, inverse, reduced, rate_lon):
    solved = lon_panels(values, inverse)
    bounds = jnp.einsum("lsrk,lmk->lsrm", lon_ends(solved), reduced, precision=highest)
    pairs = bounds.reshape(bounds.shape[:3] + (-1, 2))
    prev_last = jnp.roll(pairs[..., 1], 1, axis=-1)
    next_first = jnp.roll(pairs[..., 0], -1, axis=-1)
    return lon_finish(solved, prev_last, next_first, inverse, rate_lon)


def lat_panels(values, inverse):
    panel = inverse.shape[1]
    dims = values.shape
    split = values.reshape((dims[0], dims[1], dims[2] // panel, panel, dims[3]))
    return jnp.einsum("lscqw,lpq->lscpw", split, inverse, precision=highest)


def lat_ends(solved):
    paired = jnp.stack((solved[:, :, :, 0, :], solved[:, :, :, -1, :]), axis=3)
    return paired.reshape((paired.shape[0], paired.shape[1], -1, paired.shape[4]))


def lat_shifted(pairs):
    first_end = pairs[:, :, :, 0, :]
    last_end = pairs[:, :, :, 1, :]
    zero_row = jnp.zeros_like(last_end[:, :, :1])
    prev_last = jnp.concatenate((zero_row, last_end[:, :, :-1]), axis=2)
    next_first = jnp.concatenate((first_end[:, :, 1:], zero_row), axis=2)
    return (prev_last, next_first)


def lat_finish(solved, prev_last, next_first, inverse, rate_lat):
    left_col = inverse[:, None, None, :, 0][..., None]
    right_col = inverse[:, None, None, :, -1][..., None]
    scale = rate_lat[:, None, None, None, None]
    result = solved + scale * (
        prev_last[:, :, :, None, :] * left_col + next_first[:, :, :, None, :] * right_col
    )
    dims = result.shape
    return result.reshape((dims[0], dims[1], dims[2] * dims[3], dims[4]))


def lat_solve(values, inverse, reduced, rate_lat):
    solved = lat_panels(values, inverse)
    bounds = jnp.einsum("lskw,lmk->lsmw", lat_ends(solved), reduced, precision=highest)
    dims = bounds.shape
    pairs = bounds.reshape((dims[0], dims[1], -1, 2, dims[3]))
    prev_last, next_first = lat_shifted(pairs)
    return lat_finish(solved, prev_last, next_first, inverse, rate_lat)


def extend_block(values):
    wide = with_halo(values, (("lon", 3),), 1, True)
    return with_halo(wide, (("lat", 2),), 1, False)


def lon_lines_solve(values, inverse, reduced, rate_lon):
    finished = lon_solve(
        lax.all_to_all(values, "lon", split_axis=2, concat_axis=3, tiled=True),
        inverse,
        reduced,
        rate_lon,
    )
    return lax.all_to_all(finished, "lon", split_axis=3, concat_axis=2, tiled=True)


def lat_lines_solve(values, inverse, reduced, rate_lat):
    finished = lat_solve(
        lax.all_to_all(values, "lat", split_axis=3, concat_axis=2, tiled=True),
        inverse,
        reduced,
        rate_lat,
    )
    return lax.all_to_all(finished, "lat", split_axis=2, concat_axis=3, tiled=True)


def shards(ensemble, cross_mix, sea_mask, level_rates, panel_inverse, reduced_lon, reduced_lat):
    sea_float = sea_mask.astype(jnp.float32)[None, None]
    mixing = cross_mix[:, None]
    rate_lon = level_rates[0]
    rate_lat = level_rates[1]
    scale_lon = rate_lon[:, None, None, None]
    scale_lat = rate_lat[:, None, None, None]
    inverse_lon = panel_inverse[0]
    inverse_lat = panel_inverse[1]

    def solve_lon(values):
        return lon_lines_solve(values, inverse_lon, reduced_lon, rate_lon)

    def solve_lat(values):
        return lat_lines_solve(values, inverse_lat, reduced_lat, rate_lat)

    current = ensemble
    for repeat in range(STEPS):
        along_lon, along_lat, diagonal_diff = explicit_terms(extend_block(current))
        start_value = sea_float * (
            current
            + mixing * diagonal_diff
            + 2.0 * scale_lon * along_lon
            + 2.0 * scale_lat * along_lat
        )
        first_lon = solve_lon(start_value - scale_lon * along_lon)
        first_lat = solve_lat(first_lon - scale_lat * along_lat)
        correction = cross_term(extend_block(first_lat - current))
        corrected = start_value + 0.5 * mixing * correction
        second_lon = solve_lon(corrected - scale_lon * along_lon)
        second_lat = solve_lat(second_lon - scale_lat * along_lat)
        current = sea_float * second_lat
    return current


def solution(mesh):
    in_specs = (
        P(None, None, "lat", "lon"),
        P(None, "lat", "lon"),
        P("lat", "lon"),
        P(),
        P(),
        P(),
        P(),
    )
    out_specs = P(None, None, "lat", "lon")
    return jax.shard_map(shards, mesh=mesh, in_specs=in_specs, out_specs=out_specs, check_vma=False)
```

profile of v0, /device:TPU:1, one launch (start us, length us, event | category | flops | bytes accessed | tf_op | source)
XLA Modules:
  0.0 1258.5 jit_solution(113004368854663224)
XLA Ops:
  44.8 26.1 %all-to-all-done = f32[2,1,128,2048]{3,0,1,2:T(2,128)} async-done(((f32[2,1,128,2048]{3,0,1,2:T(2,128)}), f32[2,1,128,2048]{3,0,1,2:T(2,128)}, u32[]{:S(2)}, u32[]{:S(2)}) %all-to-all-start) | async-done | bytes 2097184 | tf_op jit(solution)/shard_map/all_to_all | solution.py:118
  103.3 24.7 %reshape.408 = f32[8,1,65536]{2,1,0:T(1,128)} reshape(f32[16384,1,2,16]{3,2,1,0:T(2,128)} %bitcast.331) | data formatting | bytes 4194304
  128.0 30.0 %all_to_all.264 = f32[8,1,65536]{2,1,0:T(1,128)} all-to-all(f32[8,1,65536]{2,1,0:T(1,128)} %reshape.408), channel_id=1, replica_groups=mesh['lat'=16,'lon'=8] {'lon'}, dimensions={0} | all-to-all | bytes 4194304 | tf_op jit(solution)/shard_map/all_to_all | solution.py:123
  167.0 31.9 %reshape.409 = f32[16384,1,2,16]{3,2,1,0:T(2,128)} reshape(f32[8,65536]{1,0:T(8,128)} %reduce.8) | data formatting | bytes 4194304
  237.9 28.4 %all-to-all-done.2 = f32[2,1,128,2048]{2,0,1,3:T(2,128)} async-done(((f32[2,1,128,2048]{2,0,1,3:T(2,128)}), f32[2,1,128,2048]{2,0,1,3:T(2,128)}, u32[]{:S(2)}, u32[]{:S(2)}) %all-to-all-start.2) | async-done | bytes 2097184 | tf_op jit(solution)/shard_map/all_to_all | solution.py:128
  282.6 33.5 %all_to_all.265 = f32[2,1,2048,128]{3,0,1,2:T(2,128)S(1)} all-to-all(f32[2,1,2048,128]{3,0,1,2:T(2,128)S(1)} %copy.178), channel_id=1, replica_groups=mesh['lat'=16,'lon'=8] {'lat'}, dimensions={2} | all-to-all | bytes 4194304 | tf_op jit(solution)/shard_map/all_to_all | solution.py:133
  355.9 28.1 %all_to_all.266 = f32[2,1,128,2048]{3,0,1,2:T(2,128)S(1)} all-to-all(f32[2,1,128,2048]{3,0,1,2:T(2,128)S(1)} %copy.181), channel_id=1, replica_groups=mesh['lat'=16,'lon'=8] {'lon'}, dimensions={2} | all-to-all | bytes 4194304 | tf_op jit(solution)/shard_map/all_to_all | solution.py:118
  414.9 24.7 %reshape.410 = f32[8,1,65536]{2,1,0:T(1,128)} reshape(f32[16384,1,2,16]{3,2,1,0:T(2,128)} %bitcast.333) | data formatting | bytes 4194304
  439.6 28.7 %all_to_all.267 = f32[8,1,65536]{2,1,0:T(1,128)} all-to-all(f32[8,1,65536]{2,1,0:T(1,128)} %reshape.410), channel_id=1, replica_groups=mesh['lat'=16,'lon'=8] {'lon'}, dimensions={0} | all-to-all | bytes 4194304 | tf_op jit(solution)/shard_map/all_to_all | solution.py:123
  476.7 31.9 %reshape.411 = f32[16384,1,2,16]{3,2,1,0:T(2,128)} reshape(f32[8,65536]{1,0:T(8,128)} %reduce.9) | data formatting | bytes 4194304
  538.3 37.9 %all_to_all.268 = f32[2,1,128,2048]{2,0,1,3:T(2,128)} all-to-all(f32[2,1,128,2048]{2,0,1,3:T(2,128)} %copy.195), channel_id=1, replica_groups=mesh['lat'=16,'lon'=8] {'lat'}, dimensions={3} | all-to-all | bytes 4194304 | tf_op jit(solution)/shard_map/all_to_all | solution.py:128
  592.4 31.8 %all_to_all.269 = f32[2,1,2048,128]{3,0,1,2:T(2,128)S(1)} all-to-all(f32[2,1,2048,128]{3,0,1,2:T(2,128)S(1)} %copy.200), channel_id=1, replica_groups=mesh['lat'=16,'lon'=8] {'lat'}, dimensions={2} | all-to-all | bytes 4194304 | tf_op jit(solution)/shard_map/all_to_all | solution.py:133
  669.0 28.4 %all_to_all.270 = f32[2,1,128,2048]{3,0,1,2:T(2,128)S(1)} all-to-all(f32[2,1,128,2048]{3,0,1,2:T(2,128)S(1)} %copy.202), channel_id=1, replica_groups=mesh['lat'=16,'lon'=8] {'lon'}, dimensions={2} | all-to-all | bytes 4194304 | tf_op jit(solution)/shard_map/all_to_all | solution.py:118
  728.3 24.8 %reshape.412 = f32[8,1,65536]{2,1,0:T(1,128)} reshape(f32[16384,1,2,16]{3,2,1,0:T(2,128)} %bitcast.335) | data formatting | bytes 4194304
  753.1 29.0 %all_to_all.271 = f32[8,1,65536]{2,1,0:T(1,128)} all-to-all(f32[8,1,65536]{2,1,0:T(1,128)} %reshape.412), channel_id=1, replica_groups=mesh['lat'=16,'lon'=8] {'lon'}, dimensions={0} | all-to-all | bytes 4194304 | tf_op jit(solution)/shard_map/all_to_all | solution.py:123
  790.6 32.1 %reshape.413 = f32[16384,1,2,16]{3,2,1,0:T(2,128)} reshape(f32[8,65536]{1,0:T(8,128)} %reduce.10) | data formatting | bytes 4194304
  854.5 36.3 %all_to_all.272 = f32[2,1,128,2048]{2,0,1,3:T(2,128)} all-to-all(f32[2,1,128,2048]{2,0,1,3:T(2,128)} %copy.216), channel_id=1, replica_groups=mesh['lat'=16,'lon'=8] {'lat'}, dimensions={3} | all-to-all | bytes 4194304 | tf_op jit(solution)/shard_map/all_to_all | solution.py:128
  907.1 31.8 %all_to_all.273 = f32[2,1,2048,128]{3,0,1,2:T(2,128)S(1)} all-to-all(f32[2,1,2048,128]{3,0,1,2:T(2,128)S(1)} %copy.221), channel_id=1, replica_groups=mesh['lat'=16,'lon'=8] {'lat'}, dimensions={2} | all-to-all | bytes 4194304 | tf_op jit(solution)/shard_map/all_to_all | solution.py:133
  980.5 28.4 %all_to_all.274 = f32[2,1,128,2048]{3,0,1,2:T(2,128)S(1)} all-to-all(f32[2,1,128,2048]{3,0,1,2:T(2,128)S(1)} %copy.223), channel_id=1, replica_groups=mesh['lat'=16,'lon'=8] {'lon'}, dimensions={2} | all-to-all | bytes 4194304 | tf_op jit(solution)/shard_map/all_to_all | solution.py:118
  1039.7 24.7 %reshape.414 = f32[8,1,65536]{2,1,0:T(1,128)} reshape(f32[16384,1,2,16]{3,2,1,0:T(2,128)} %bitcast.337) | data formatting | bytes 4194304
  1064.5 29.0 %all_to_all.275 = f32[8,1,65536]{2,1,0:T(1,128)} all-to-all(f32[8,1,65536]{2,1,0:T(1,128)} %reshape.414), channel_id=1, replica_groups=mesh['lat'=16,'lon'=8] {'lon'}, dimensions={0} | all-to-all | bytes 4194304 | tf_op jit(solution)/shard_map/all_to_all | solution.py:123
  1101.9 31.8 %reshape.415 = f32[16384,1,2,16]{3,2,1,0:T(2,128)} reshape(f32[8,65536]{1,0:T(8,128)} %reduce.11) | data formatting | bytes 4194304
  1165.6 36.3 %all_to_all.276 = f32[2,1,128,2048]{2,0,1,3:T(2,128)} all-to-all(f32[2,1,128,2048]{2,0,1,3:T(2,128)} %copy.237), channel_id=1, replica_groups=mesh['lat'=16,'lon'=8] {'lat'}, dimensions={3} | all-to-all | bytes 4194304 | tf_op jit(solution)/shard_map/all_to_all | solution.py:128
  1218.1 31.8 %all_to_all.277 = f32[2,1,2048,128]{3,0,1,2:T(2,128)S(1)} all-to-all(f32[2,1,2048,128]{3,0,1,2:T(2,128)S(1)} %copy.242), channel_id=1, replica_groups=mesh['lat'=16,'lon'=8] {'lat'}, dimensions={2} | all-to-all | bytes 4194304 | tf_op jit(solution)/shard_map/all_to_all | solution.py:133
  (238 shorter events, 535.3 us)
Async XLA Ops:
  0.0 84.1 %copy-start = (f32[2,256,256]{2,1,0:T(8,128)S(1)}, f32[2,256,256]{2,1,0:T(8,128)}, u32[]{:S(2)}) copy-start(f32[2,256,256]{2,1,0:T(8,128)} %param.12) | copy-start | bytes 1572868
  1.1 7.8 collective-permute-start.1
  6.8 5.9 collective-permute-start
  7.6 15.5 %copy-start.12 = (f32[2,2]{1,0:T(2,128)S(1)}, f32[2,2]{1,0:T(2,128)}, u32[]{:S(2)}) copy-start(f32[2,2]{1,0:T(2,128)} %param.10) | copy-start | bytes 52
  15.7 7.4 copy-start.5
  15.7 8.7 copy-start.1
  15.8 8.7 collective-permute-start.2
  20.0 4.4 collective-permute-start.3
  39.8 4.7 copy-start.10
  39.8 31.0 %all-to-all-start = ((f32[2,1,128,2048]{3,0,1,2:T(2,128)}), f32[2,1,128,2048]{3,0,1,2:T(2,128)}, u32[]{:S(2)}, u32[]{:S(2)}) async-start(f32[2,1,128,2048]{3,0,1,2:T(2,128)} %copy.159), calls=%async_computation | async-start | bytes 4194304 | tf_op jit(solution)/shard_map/all_to_all | solution.py:118
  228.7 37.7 %all-to-all-start.2 = ((f32[2,1,128,2048]{2,0,1,3:T(2,128)}), f32[2,1,128,2048]{2,0,1,3:T(2,128)}, u32[]{:S(2)}, u32[]{:S(2)}) async-start(f32[2,1,128,2048]{2,0,1,3:T(2,128)} %copy.173), calls=%async_computation.2 | async-start | bytes 4194304 | tf_op jit(solution)/shard_map/all_to_all | solution.py:128
  270.4 3.7 copy-start.11
  325.2 3.9 collective-permute-start.5
  325.6 5.9 collective-permute-start.4
  336.6 6.4 collective-permute-start.6
  341.0 3.1 collective-permute-start.7
  632.7 4.1 collective-permute-start.9
  634.8 5.9 collective-permute-start.8
  645.8 6.3 collective-permute-start.10
  650.2 3.1 collective-permute-start.11
  948.2 3.9 collective-permute-start.13
  950.1 5.9 collective-permute-start.12
  961.1 6.3 collective-permute-start.14
  965.5 3.1 collective-permute-start.15
  (7 other events, 9.3 us)
where the time goes:
time: 1270 us; the launch traced here: 1260 us
  local copies, waits for them, and re-layouts  524 us (41%)
  blocking collectives  441 us (35%)
  other arithmetic  130 us (10%)
  waiting for transfers between devices  79.7 us (6%)
  starting transfers between devices  51.2 us (4%)
  matrix products  31.6 us (2%)
    unnamed x34, local copies, waits for them, and re-layouts  236 us
    all_to_all x4, blocking collectives, lat_lines_solve(): lax.all_to_all(finished, 'lat', split_axis=2, concat_axis=3, tiled=True)  129 us
    all_to_all x4, blocking collectives, lon_lines_solve(): lax.all_to_all(finished, 'lon', split_axis=3, concat_axis=2, tiled=True)  117 us
    all_to_all x3, blocking collectives, lat_lines_solve(): lax.all_to_all(values, 'lat', split_axis=3, concat_axis=2, tiled=True)  111 us
    all_to_all x5, local copies, waits for them, and re-layouts, lon_lines_solve(): lax.all_to_all(finished, 'lon', split_axis=3, concat_axis=2, tiled=True)  86.9 us
    all_to_all x3, blocking collectives, lon_lines_solve(): lax.all_to_all(values, 'lon', split_axis=2, concat_axis=3, tiled=True)  84.8 us
    reshape x4, local copies, waits for them, and re-layouts, lon_finish(): return result.reshape(result.shape[:3] + (-1,))  57.4 us
    all_to_all x4, other arithmetic, lon_lines_solve(): lax.all_to_all(finished, 'lon', split_axis=3, concat_axis=2, tiled=True)  33.9 us
  transfers between devices with their start and end apart: 18, of which 13 were waited for; matrix products, arithmetic and copies ran while one was open for 0% of the time, Pallas kernels for 0%

commit v1 on v0

v1 whole, which is shorter than its diff:
```python
import functools

import jax
import jax.numpy as jnp
from jax import lax
from jax.experimental import pallas as pl
from jax.experimental.pallas import tpu as pltpu
from jax.sharding import PartitionSpec as P

LEV, ROWS, COLS = 2, 128, 2048
KT, TT, SS, LN = 16, 16, 8, 128
NLAT_DEV, NLON_DEV = 16, 8
NLAT, NLON = ROWS * NLAT_DEV, COLS * NLON_DEV
F32, BF16 = jnp.float32, jnp.bfloat16
VM = pl.BlockSpec(memory_space=pltpu.VMEM)
SM = pl.BlockSpec(memory_space=pltpu.SMEM)
HB = pl.BlockSpec(memory_space=pl.ANY)
PARAMS = pltpu.CompilerParams(vmem_limit_bytes=40 * 1024 * 1024)

L_P, L_LQ, L_Q, L_CQ, L_CQL, L_CP, L_GQ, L_GP = range(8)
PK = 40


def shape(*dims, dtype=F32):
    return jax.ShapeDtypeStruct(dims, dtype)


def iota(dims, axis):
    return lax.broadcasted_iota(jnp.int32, dims, axis)


def fiota(dims, axis):
    return iota(dims, axis).astype(F32)


class Rates:
    def __init__(self, par, level):
        self.t1, self.t2, self.a1, self.a2, self.c1, self.c2 = (par[8 * level + i] for i in range(6))


def position(par):
    return par[16], par[17]


def split3(x):
    high = x.astype(BF16)
    rest = x - high.astype(F32)
    mid = rest.astype(BF16)
    return high, mid, (rest - mid.astype(F32)).astype(BF16)


def dot(x, y):
    return jnp.dot(x, y, preferred_element_type=F32)


def tables_kernel(par, u_hbm, m_hbm, k_hbm, ul, ml, kl, w1, w3, k1, k3, et, lt, el, su, sm, sk, sem):
    copies = []
    for l in range(LEV):
        copies.append([pltpu.make_async_copy(u_hbm.at[l, :, pl.ds(k * LN, LN)], su.at[l, k], sem.at[l]) for k in range(KT)])
    for l in range(LEV):
        copies.append([pltpu.make_async_copy(m_hbm.at[l, :, pl.ds(k * LN, LN)], sm.at[l, k], sem.at[2 + l]) for k in range(KT)])
    copies.append([pltpu.make_async_copy(k_hbm.at[:, pl.ds(k * LN, LN)], sk.at[k], sem.at[4]) for k in range(KT)])
    for group in copies:
        for c in group:
            c.start()
    i_pos, _ = position(par)
    for l in range(LEV):
        r = Rates(par, l)
        dist = jnp.abs(fiota((LN, LN), 0) - fiota((LN, LN), 1))
        high, mid, low = split3(r.c1 * jnp.exp(-r.t1 * dist))
        k1[l] = jnp.concatenate([high, mid], axis=1)
        k3[l] = low
        lane = iota((LN, LN), 1)
        row = fiota((LN, LN), 0)
        slot = lane % 32
        rising = ((lane < 96) & (slot >= 16)) | (lane == 97)
        base = jnp.exp(-r.t1 * jnp.where(rising, row, (LN - 1) - row))

        def weights(k, carry):
            kf = k.astype(F32)
            pick = jnp.where((lane < 96) & (slot % 16 == k), 1.0, 0.0)
            pick = jnp.where(lane == 96, jnp.exp(-r.t1 * (LN * (KT - 1 - kf))), pick)
            pick = jnp.where(lane == 97, jnp.exp(-r.t1 * (LN * kf)), pick)
            high, mid, low = split3(base * pick)
            w1[l, k] = jnp.concatenate([high, mid], axis=1)
            w3[l, k] = low
            return carry

        lax.fori_loop(0, KT, weights, 0)
        slot = iota((32, LN), 0)
        col = fiota((32, LN), 1)
        own = (slot % 16).astype(F32)
        for k in range(KT):
            gap = jnp.where(slot < 16, k - own, own - k)
            power = (gap - 1) * LN + jnp.where(slot < 16, col + 1, LN - col)
            value = jnp.where(gap > 0, r.c1 * jnp.exp(-r.t1 * jnp.maximum(power, 0.0)), 0.0)
            high, mid, low = split3(value)
            zero = jnp.zeros_like(high)
            et[l, :, pl.ds(k * LN, LN)] = jnp.concatenate([high, mid, low, zero, high, mid, high, zero], axis=0)
        lane_f = fiota((SS, LN), 1)
        for k in range(KT):
            el[l, 0, k] = r.c1 * jnp.exp(-r.t1 * (k * LN + lane_f + 1.0))
            el[l, 1, k] = r.c1 * jnp.exp(-r.t1 * (COLS - k * LN - lane_f))
        sub = fiota((SS, LN), 0)
        scale = r.c2 / (1.0 - jnp.exp(jnp.full((SS, LN), -2.0 * (NLAT + 1), F32) * r.t2))
        for t in range(TT):
            local = sub * TT + t
            index = local + i_pos * ROWS
            p = 1.0 - jnp.exp(-2.0 * r.t2 * (index + 1.0))
            q = 1.0 - jnp.exp(-2.0 * r.t2 * (NLAT - index))
            lt[l, L_P, t] = p
            lt[l, L_Q, t] = q
            lt[l, L_LQ, t] = q * jnp.exp(jnp.full((SS, LN), -float(t), F32) * r.t2)
            lt[l, L_CQ, t] = scale * q
            lt[l, L_CQL, t] = scale * q * jnp.exp(jnp.full((SS, LN), -float(t + 1), F32) * r.t2)
            lt[l, L_CP, t] = scale * p
            lt[l, L_GQ, t] = scale * q * jnp.exp(-r.t2 * (local + 1.0))
            lt[l, L_GP, t] = scale * p * jnp.exp(-r.t2 * (ROWS - local))
    for group in copies:
        for c in group:
            c.wait()

    def move(k, carry):
        for t in range(TT):
            for l in range(LEV):
                ul[l, k, t] = su[l, k, pl.ds(t, SS, stride=TT), :]
                ml[l, k, t] = sm[l, k, pl.ds(t, SS, stride=TT), :]
            kl[k, t] = sk[k, pl.ds(t, SS, stride=TT), :].astype(F32)
        return carry

    lax.fori_loop(0, KT, move, 0)


def right_left(tiles, ext):
    lane = iota((1, SS, LN), 2)
    right = pltpu.roll(tiles, LN - 1, 2)
    left = pltpu.roll(tiles, 1, 2)
    if ext is None:
        beyond_right = before_left = jnp.zeros((1, SS, LN), F32)
    else:
        beyond_right = pltpu.roll(ext, LN - 2, 1)[None]
        before_left = ext[None]
    next_right = jnp.concatenate([right[1:], beyond_right], axis=0)
    prev_left = jnp.concatenate([before_left, left[:-1]], axis=0)
    return jnp.where(lane == LN - 1, next_right, right), jnp.where(lane == 0, prev_left, left)


def north_of(last, halo):
    return jnp.where(iota(last.shape, last.ndim - 2) == 0, halo, pltpu.roll(last, 1, last.ndim - 2))


def south_of(first, halo):
    return jnp.where(iota(first.shape, first.ndim - 2) == SS - 1, halo, pltpu.roll(first, SS - 1, first.ndim - 2))


def down_scan(x, t2):
    sub = iota(x.shape, x.ndim - 2)
    x = jnp.where(sub >= 1, pltpu.roll(x, 1, x.ndim - 2), 0.0)
    for step in (1, 2, 4):
        factor = jnp.exp(jnp.full((SS, LN), -float(TT * step), F32) * t2)
        x = x + factor * jnp.where(sub >= step, pltpu.roll(x, step, x.ndim - 2), 0.0)
    return x


def up_scan(x, t2):
    sub = iota(x.shape, x.ndim - 2)
    x = jnp.where(sub < SS - 1, pltpu.roll(x, SS - 1, x.ndim - 2), 0.0)
    for step in (1, 2, 4):
        factor = jnp.exp(jnp.full((SS, LN), -float(TT * step), F32) * t2)
        x = x + factor * jnp.where(sub < SS - step, pltpu.roll(x, SS - step, x.ndim - 2), 0.0)
    return x


def chunk_ends(last, acc, t2):
    carry_down = down_scan(last, t2)
    carry_up = up_scan(acc, t2)
    step = jnp.exp(jnp.full((SS, LN), -float(TT), F32) * t2)
    phi = (last + step * carry_down)[..., SS - 1 : SS, :]
    psi = (acc + step * carry_up)[..., 0:1, :]
    return carry_down, carry_up, jnp.broadcast_to(phi, last.shape), jnp.broadcast_to(psi, last.shape)


def lam2(t2):
    return jnp.exp(jnp.full((SS, LN), -1.0, F32) * t2)


def local_solve(par, qs, xs, ss, w1, w3, k1, k3, et, lt, zl, phi, with_p):
    sums = []
    for l in range(LEV):
        r = Rates(par, l)

        def tile(k, ab):
            high, mid, low = split3(qs[l, k].reshape(ROWS, LN))
            lhs1 = jnp.concatenate([high, mid], axis=1)
            lhs2 = jnp.concatenate([low, high], axis=1)
            kk = k1[l]
            one = dot(lhs1, jnp.concatenate([kk, kk], axis=0))
            two = dot(lhs2, jnp.concatenate([kk[:, :LN], k3[l]], axis=0))
            x = (one[:, :LN] + one[:, LN:] + two).reshape(TT, SS, LN)
            xs[l, k] = xs[l, k] + x if with_p else x
            ww = w1[l, k]
            one = dot(lhs1, jnp.concatenate([ww, ww], axis=0))
            two = dot(lhs2, jnp.concatenate([ww[:, :LN], w3[l, k]], axis=0))
            return ab + (one[:, :LN] + one[:, LN:] + two)

        ab = lax.fori_loop(0, KT, tile, jnp.zeros((ROWS, LN), F32))
        sums.append(ab)
        high, mid, low = split3(ab)
        lane = iota((ROWS, LN), 1)
        second = jnp.where(lane < 64, mid.astype(F32), low.astype(F32)).astype(BF16)
        lhs = jnp.concatenate([high, second], axis=1)
        for k in range(0, KT, 2):
            fix = dot(lhs, et[l, :, pl.ds(k * LN, 2 * LN)])
            xs[l, k] += fix[:, :LN].reshape(TT, SS, LN)
            xs[l, k + 1] += fix[:, LN:].reshape(TT, SS, LN)

        lam = lam2(r.t2)

        def down(t, carry):
            s, acc = carry
            x = xs[l, :, t]
            s = lam * s + lt[l, L_P, t] * x
            ss[:, t] = s
            return s, acc + lt[l, L_LQ, t] * x

        zero = jnp.zeros((KT, SS, LN), F32)
        last, acc = lax.fori_loop(0, TT, down, (zero, zero))
        carry_down, carry_up, phi_l, psi_l = chunk_ends(last, acc, r.t2)
        phi[l, 0] = phi_l
        phi[l, 1] = psi_l

        def up(i, u):
            t = TT - 1 - i
            zl[l, :, t] = lt[l, L_CQ, t] * ss[:, t] + lt[l, L_CQL, t] * carry_down + lt[l, L_CP, t] * u
            return lam * (u + lt[l, L_Q, t] * xs[l, :, t])

        lax.fori_loop(0, TT, up, lam * carry_up)
    return sums


def explicit(r, before, here, after, ext_here, ext_diff, mixing, mask):
    east, west = right_left(here, ext_here)
    lon = east + west - 2.0 * here
    lat = after + before - 2.0 * here
    east, west = right_left(after - before, ext_diff)
    q = mask * (here + mixing * (east - west) + (2.0 * r.a1) * lon + (2.0 * r.a2) * lat) - r.a1 * lon
    return q, -r.a2 * lat


def end_columns(first, last):
    lane = iota((ROWS, LN), 1)
    turned = jnp.where(lane < 64, first, last).T
    return turned[0:1], turned[LN - 1 : LN]


def first_kernel(par, ul, ml, kl, north, south, w1, w3, k1, k3, et, lt, zl, phi, msg, uh, kh, qs, xs, ss):
    def spread(ref, row):
        return jnp.stack([jnp.broadcast_to(ref[row, k : k + 1, :], (SS, LN)) for k in range(KT)])

    for side, ref in ((0, north), (1, south)):
        kh[side, :KT] = spread(ref, 2)
    for l in range(LEV):
        r = Rates(par, l)
        uh[l, 0, :KT] = spread(north, l)
        uh[l, 1, :KT] = spread(south, l)

        def rows(t, before, after):
            q, p = explicit(r, before, ul[l, :, t], after, None, None, ml[l, :, t], kl[:, t])
            qs[l, :, t] = q
            xs[l, :, t] = p

        rows(0, north_of(ul[l, :, TT - 1], uh[l, 0, :KT]), ul[l, :, 1])

        def body(t, carry):
            rows(t, ul[l, :, t - 1], ul[l, :, t + 1])
            return carry

        lax.fori_loop(1, TT - 1, body, 0)
        rows(TT - 1, ul[l, :, TT - 2], south_of(ul[l, :, 0], uh[l, 1, :KT]))
    sums = local_solve(par, qs, xs, ss, w1, w3, k1, k3, et, lt, zl, phi, True)
    parts = []
    for l in range(LEV):
        parts.append(sums[l].T[96:98])
    for l in range(LEV):
        parts.extend(end_columns(ul[l, 0].reshape(ROWS, LN), ul[l, KT - 1].reshape(ROWS, LN)))
    for l in range(LEV):
        parts.extend(end_columns(ml[l, 0].reshape(ROWS, LN), ml[l, KT - 1].reshape(ROWS, LN)))
    parts.extend(end_columns(kl[0].reshape(ROWS, LN), kl[KT - 1].reshape(ROWS, LN)))
    lane = iota((1, LN), 1)
    for row in range(3):
        n0, s0 = north[row, 0:1, :], south[row, 0:1, :]
        n1, s1 = north[row, KT - 1 : KT, :], south[row, KT - 1 : KT, :]
        parts.append(jnp.where(lane == 0, n0, pltpu.roll(s0, 1, 1)))
        parts.append(jnp.where(lane == LN - 1, n1, pltpu.roll(s1, LN - 1, 1)))
    parts.append(jnp.zeros((4, LN), F32))
    block = jnp.concatenate(parts, axis=0)
    for j in range(NLON_DEV):
        msg[j] = block


def row_after(x, halo):
    lane = iota(x.shape, 1)
    y = jnp.where(lane >= LN - SS, pltpu.roll(x, LN - SS - 1, 1), pltpu.roll(x, LN - SS, 1))
    return jnp.where(lane == LN - 1, halo, y)


def row_before(x, halo):
    lane = iota(x.shape, 1)
    y = jnp.where(lane < SS, pltpu.roll(x, SS + 1, 1), pltpu.roll(x, SS, 1))
    return jnp.where(lane == 0, halo, y)


def lane_value(x, index):
    return jnp.sum(jnp.where(iota(x.shape, x.ndim - 1) == index, x, 0.0), axis=-1, keepdims=True)


def as_tile(rows):
    count = sum(r.shape[0] for r in rows)
    return jnp.concatenate(rows + [jnp.zeros((LN - count, LN), F32)], axis=0).T.reshape(TT, SS, LN)


def carry_kernel(first, *refs):
    if first:
        par, got, phi, lt, el, out, pack, ze, ux, kx, uhx, khx = refs
    else:
        par, got, phi, px, lt, el, out, pack, ze = refs
    i_pos, j_pos = position(par)
    peer = fiota((NLON_DEV, LN), 0)
    mine = peer == j_pos
    fluxes = []
    ext = []
    if first:
        kw = pltpu.roll(got[:, 13, :], 1, 0)
        ke = pltpu.roll(got[:, 12, :], NLON_DEV - 1, 0)
        kw_end = pltpu.roll(got[:, 19, :], 1, 0)
        ke_end = pltpu.roll(got[:, 18, :], NLON_DEV - 1, 0)

        def own(x):
            return jnp.sum(jnp.where(mine, x, 0.0), axis=0, keepdims=True)

        def corners(west_end, east_end):
            lane = iota((1, LN), 1)
            w, e = own(west_end), own(east_end)
            w_n, w_s = lane_value(w, LN - 1), lane_value(w, LN - 2)
            e_n, e_s = lane_value(e, 0), lane_value(e, 1)
            pick = lambda a, b: jnp.broadcast_to(jnp.where(lane == 0, a, jnp.where(lane == 1, b, 0.0)), (SS, LN))
            return pick(w_n, e_n), pick(w_s, e_s)

        khx[0], khx[1] = corners(kw_end, ke_end)
        kx[...] = as_tile([own(kw), own(ke)])
    for l in range(LEV):
        r = Rates(par, l)
        a, b = got[:, 2 * l, :], got[:, 2 * l + 1, :]
        one = jnp.full((NLON_DEV, LN), 1.0, F32)
        if first:
            uw = pltpu.roll(got[:, 5 + 2 * l, :], 1, 0)
            ue = pltpu.roll(got[:, 4 + 2 * l, :], NLON_DEV - 1, 0)
            uw_end = pltpu.roll(got[:, 15 + 2 * l, :], 1, 0)
            ue_end = pltpu.roll(got[:, 14 + 2 * l, :], NLON_DEV - 1, 0)
            w_up = row_before(uw, jnp.sum(jnp.where(iota(uw.shape, 1) == LN - 1, uw_end, 0.0), axis=1, keepdims=True))
            w_dn = row_after(uw, jnp.sum(jnp.where(iota(uw.shape, 1) == LN - 2, uw_end, 0.0), axis=1, keepdims=True))
            e_up = row_before(ue, jnp.sum(jnp.where(iota(ue.shape, 1) == 0, ue_end, 0.0), axis=1, keepdims=True))
            e_dn = row_after(ue, jnp.sum(jnp.where(iota(ue.shape, 1) == 1, ue_end, 0.0), axis=1, keepdims=True))
            m0, mn, k0, kn = got[:, 8 + 2 * l, :], got[:, 9 + 2 * l, :], got[:, 12, :], got[:, 13, :]
            h0 = k0 * (m0 * (w_up - w_dn) + 2.0 * r.a1 * uw) - r.a1 * uw
            hn = kn * (mn * (e_dn - e_up) + 2.0 * r.a1 * ue) - r.a1 * ue
            far = jnp.exp(-(COLS - 1.0) * r.t1 * one)
            a = a + far * h0 + hn
            b = b + h0 + far * hn
        whole = 1.0 - jnp.exp(-float(NLON) * r.t1 * one)
        back = j_pos - peer - 1.0
        back = jnp.where(back < 0, back + NLON_DEV, back)
        ahead = peer - j_pos - 1.0
        ahead = jnp.where(ahead < 0, ahead + NLON_DEV, ahead)
        left = jnp.sum(a * (jnp.exp(-r.t1 * COLS * back) / whole), axis=0, keepdims=True)
        right = jnp.sum(b * (jnp.exp(-r.t1 * COLS * ahead) / whole), axis=0, keepdims=True)
        a = jnp.sum(jnp.where(mine, a, 0.0), axis=0, keepdims=True)
        b = jnp.sum(jnp.where(mine, b, 0.0), axis=0, keepdims=True)
        lam = jnp.exp(-r.t1 * jnp.full((1, LN), 1.0, F32))
        far = jnp.exp(-(COLS + 1.0) * r.t1 * jnp.full((1, LN), 1.0, F32))
        xw = r.c1 * (left + lam * b + far * right)
        xe = r.c1 * (right + lam * a + far * left)
        if first:
            pw = -r.a2 * (w_dn + w_up - 2.0 * uw)
            pe = -r.a2 * (e_dn + e_up - 2.0 * ue)
            xw = xw + own(pw)
            xe = xe + own(pe)
            left = left + own(h0) / lam
            right = right + own(hn) / lam
            ux[l] = as_tile([own(uw), own(ue)])
            uhx[l, 0], uhx[l, 1] = corners(uw_end, ue_end)
        x = as_tile([xw, xe, left, right])
        if not first:
            x = x + px[l]
        ext.append(x)
    lams = [lam2(Rates(par, l).t2) for l in range(LEV)]
    zero = jnp.zeros((SS, LN), F32)
    state = [zero, zero]
    acc = [zero, zero]
    kept = [[], []]
    for t in range(TT):
        for l in range(LEV):
            state[l] = lams[l] * state[l] + lt[l, L_P, t] * ext[l][t]
            acc[l] = acc[l] + lt[l, L_LQ, t] * ext[l][t]
            kept[l].append(state[l])
    for l in range(LEV):
        r = Rates(par, l)
        carry_down, carry_up, phi_e, psi_e = chunk_ends(state[l], acc[l], r.t2)
        u = lams[l] * carry_up
        for t in range(TT - 1, -1, -1):
            ze[l, t] = lt[l, L_CQ, t] * kept[l][t] + lt[l, L_CQL, t] * carry_down + lt[l, L_CP, t] * u
            u = lams[l] * (u + lt[l, L_Q, t] * ext[l][t])
        pair = []
        for side, flux in ((0, phi_e), (1, psi_e)):
            tiles = phi[l, side] + lane_value(flux, 2) * el[l, 0] + lane_value(flux, 3) * el[l, 1]
            pair.append([tiles[k] for k in range(KT)] + [flux])
        fluxes.append(pair)
    sub = iota((SS, LN), 0)
    packed = []
    for side in (0, 1):
        rows = fluxes[0][side] + fluxes[1][side]
        rows = rows + [zero] * (PK - len(rows))
        vregs = []
        for v in range(PK // SS):
            y = rows[v * SS]
            for j in range(1, SS):
                y = jnp.where(sub == j, rows[v * SS + j], y)
            vregs.append(y)
        packed.append(jnp.concatenate(vregs, axis=0))
        pack[side] = packed[side]
    t2 = level_rows(Rates(par, 0).t2, Rates(par, 1).t2)
    for p in range(NLAT_DEV):
        away = jnp.maximum(jnp.abs(p - i_pos) - 1.0, 0.0)
        factor = jnp.exp(-(ROWS * away) * t2)
        ahead = jnp.full((PK, LN), p - i_pos, F32) > 0
        out[p] = factor * jnp.where(ahead, packed[0], packed[1])


def level_rows(low, high):
    return jnp.where(iota((PK, LN), 0) <= KT, low, high)


def arrive(par, got, pack, tb, vb, hb):
    i_pos, _ = position(par)
    zero = jnp.zeros((PK, LN), F32)
    above, below = zero, zero
    for p in range(NLAT_DEV):
        side = jnp.full((PK, LN), p - i_pos, F32)
        above = above + jnp.where(side < 0, got[p], 0.0)
        below = below + jnp.where(side > 0, got[p], 0.0)
    t2 = level_rows(Rates(par, 0).t2, Rates(par, 1).t2)
    scale = level_rows(Rates(par, 0).c2, Rates(par, 1).c2) / (1.0 - jnp.exp(-2.0 * (NLAT + 1) * t2))
    lam = jnp.exp(-t2)
    block = jnp.exp(-float(ROWS) * t2)
    start = i_pos * ROWS
    q_n = 1.0 - jnp.exp(-2.0 * t2 * (NLAT + 1.0 - start))
    p_n = 1.0 - jnp.exp(-2.0 * t2 * start)
    q_s = 1.0 - jnp.exp(-2.0 * t2 * (NLAT - ROWS - start))
    p_s = 1.0 - jnp.exp(-2.0 * t2 * (ROWS + 1.0 + start))
    north = scale * (q_n * above + p_n * lam * (pack[1] + block * below))
    south = scale * (q_s * lam * (pack[0] + block * above) + p_s * below)
    for l in range(LEV):
        for k in range(KT + 1):
            at = l * (KT + 1) + k
            wide = lambda x: jnp.broadcast_to(x[at : at + 1], (SS, LN))
            tb[l, k] = wide(above)
            vb[l, k] = wide(below)
            if hb is not None:
                hb[l, 0, k] = wide(north)
                hb[l, 1, k] = wide(south)


def solved_rows(l, t, zl, ze, el, lt, tb, vb):
    extra = ze[l, t]
    gq, gp = lt[l, L_GQ, t], lt[l, L_GP, t]
    z_left = jnp.broadcast_to(extra[:, 2:3], (SS, LN))
    z_right = jnp.broadcast_to(extra[:, 3:4], (SS, LN))
    own = zl[l, :, t] + el[l, 0] * z_left + el[l, 1] * z_right + gq * tb[l, :KT] + gp * vb[l, :KT]
    return own, extra + gq * tb[l, KT] + gp * vb[l, KT]


def send_sums(sums, msg):
    block = jnp.concatenate([s.T[96:98] for s in sums] + [jnp.zeros((4, LN), F32)], axis=0)
    for j in range(NLON_DEV):
        msg[j] = block


def half_kernel(par, got, pack, zl, ze, ul, ux, uh, uhx, ml, el, w1, w3, k1, k3, et, lt,
                y2, yx, yh, zo, phi, msg, px, tb, vb, vs, qs, xs, ss):
    arrive(par, got, pack, tb, vb, yh)
    for l in range(LEV):
        r = Rates(par, l)

        def rows(t, carry):
            own, extra = solved_rows(l, t, zl, ze, el, lt, tb, vb)
            y2[l, :, t] = own
            yx[l, t] = extra
            vs[:KT, t + 1] = own - ul[l, :, t]
            vs[KT, t + 1] = extra - ux[l, t]
            px[l, t] = jnp.zeros((SS, LN), F32)
            return carry

        lax.fori_loop(0, TT, rows, 0)
        for side, edge, at, turn in ((0, TT, 0, north_of), (1, 1, TT + 1, south_of)):
            vs[:KT, at] = turn(vs[:KT, edge], yh[l, side, :KT] - uh[l, side, :KT])
            vs[KT, at] = turn(vs[KT, edge], yh[l, side, KT] - uhx[l, side])

        def body(t, carry):
            diff = vs[:, t + 2] - vs[:, t]
            east, west = right_left(diff[:KT], diff[KT])
            qs[l, :, t] = 0.5 * ml[l, :, t] * (east - west)
            return carry

        lax.fori_loop(0, TT, body, 0)
    send_sums(local_solve(par, qs, xs, ss, w1, w3, k1, k3, et, lt, zo, phi, False), msg)


def step_kernel(par, got, pack, zl, ze, y2, yx, yh, kl, kx, kh, khx, ml, el, w1, w3, k1, k3, et, lt,
                un, unx, unh, unhx, zo, phi, msg, px, tb, vb, hb, vs, qs, xs, ss):
    arrive(par, got, pack, tb, vb, hb)
    for l in range(LEV):
        r = Rates(par, l)

        def rows(t, carry):
            own, extra = solved_rows(l, t, zl, ze, el, lt, tb, vb)
            own = kl[:, t] * (own + y2[l, :, t])
            extra = kx[t] * (extra + yx[l, t])
            un[l, :, t] = own
            unx[l, t] = extra
            vs[:KT, t + 1] = own
            vs[KT, t + 1] = extra
            return carry

        lax.fori_loop(0, TT, rows, 0)
        for side, edge, at, turn in ((0, TT, 0, north_of), (1, 1, TT + 1, south_of)):
            halo = kh[side, :KT] * (yh[l, side, :KT] + hb[l, side, :KT])
            halo_x = khx[side] * (yh[l, side, KT] + hb[l, side, KT])
            unh[l, side, :KT] = halo
            unhx[l, side] = halo_x
            vs[:KT, at] = turn(vs[:KT, edge], halo)
            vs[KT, at] = turn(vs[KT, edge], halo_x)

        def body(t, carry):
            before, here, after = vs[:, t], vs[:, t + 1], vs[:, t + 2]
            q, p = explicit(r, before[:KT], here[:KT], after[:KT], here[KT], (after - before)[KT], ml[l, :, t], kl[:, t])
            qs[l, :, t] = q
            xs[l, :, t] = p
            extra = -r.a2 * (after[KT] + before[KT] - 2.0 * here[KT])
            px[l, t] = jnp.where(iota((SS, LN), 1) < 2, extra, 0.0)
            return carry

        lax.fori_loop(0, TT, body, 0)
    send_sums(local_solve(par, qs, xs, ss, w1, w3, k1, k3, et, lt, zo, phi, True), msg)


def last_kernel(par, got, pack, zl, ze, y2, kl, el, lt, out, tb, vb, os, sem):
    arrive(par, got, pack, tb, vb, None)
    copies = []
    for l in range(LEV):

        def rows(t, carry):
            own, _ = solved_rows(l, t, zl, ze, el, lt, tb, vb)
            own = kl[:, t] * (own + y2[l, :, t])
            for k in range(KT):
                os[l, k, pl.ds(t, SS, stride=TT), :] = own[k]
            return carry

        lax.fori_loop(0, TT, rows, 0)
        for k in range(KT):
            copies.append(pltpu.make_async_copy(os.at[l, k], out.at[l, :, pl.ds(k * LN, LN)], sem.at[l]))
            copies[-1].start()
    for c in copies:
        c.wait()


FIELD = (LEV, KT, TT, SS, LN)
EXTRA = (LEV, TT, SS, LN)
HALO = (LEV, 2, KT + 1, SS, LN)
FLUX = (LEV, 2, KT, SS, LN)


def call(kernel, outs, ins, scratch=(), out_specs=None, in_specs=None):
    return pl.pallas_call(
        kernel,
        out_shape=outs,
        in_specs=in_specs or [SM] + [VM] * (len(ins) - 1),
        out_specs=out_specs or [VM] * len(outs),
        scratch_shapes=list(scratch),
        compiler_params=PARAMS,
    )(*ins)


def vmem(*dims):
    return pltpu.VMEM(dims, F32)


def halo_rows(ensemble, mask):
    at = lax.axis_index("lat")
    first = jnp.concatenate([ensemble[:, 0, 0, :], mask[0:1, :]], axis=0).reshape(3, KT, LN)
    last = jnp.concatenate([ensemble[:, 0, ROWS - 1, :], mask[ROWS - 1 :, :]], axis=0).reshape(3, KT, LN)
    even = at % 2 == 0
    pairs = [(i, i + 1) for i in range(0, NLAT_DEV, 2)]
    odd_pairs = [(i, i + 1) for i in range(1, NLAT_DEV - 1, 2)]
    both = lambda edges: edges + [(j, i) for i, j in edges]
    one = lax.ppermute(jnp.where(even, last, first), "lat", both(pairs))
    two = lax.ppermute(jnp.where(even, first, last), "lat", both(odd_pairs))
    return jnp.where(even, two, one), jnp.where(even, one, two)


def parameters(level_rates):
    a = level_rates
    half = 0.5 / jnp.sqrt(a)
    theta = 2.0 * jnp.log1p(half + half * half / (1.0 + jnp.sqrt(1.0 + half * half)))
    scale = 1.0 / jnp.sqrt(1.0 + 4.0 * a)
    zero = jnp.zeros((LEV,), F32)
    table = jnp.stack([theta[0], theta[1], a[0], a[1], scale[0], scale[1], zero, zero], axis=1).reshape(-1)
    where = jnp.stack([lax.axis_index("lat"), lax.axis_index("lon")]).astype(F32)
    return jnp.concatenate([table, where])


def exchange(values, axis):
    return lax.all_to_all(values, axis, split_axis=0, concat_axis=0, tiled=True)


def shards(ensemble, cross_mix, sea_mask, level_rates, panel_inverse, reduced_lon, reduced_lat):
    par = parameters(level_rates)
    north, south = halo_rows(ensemble, sea_mask.astype(F32))
    work = [vmem(*FIELD), vmem(*FIELD), vmem(KT, TT, SS, LN)]
    carries = [vmem(LEV, KT + 1, SS, LN), vmem(LEV, KT + 1, SS, LN)]
    diffs = vmem(KT + 1, TT + 2, SS, LN)
    ul, ml, kl, w1, w3, k1, k3, et, lt, el = call(
        tables_kernel,
        [shape(*FIELD), shape(*FIELD), shape(KT, TT, SS, LN),
         shape(LEV, KT, LN, 2 * LN, dtype=BF16), shape(LEV, KT, LN, LN, dtype=BF16),
         shape(LEV, LN, 2 * LN, dtype=BF16), shape(LEV, LN, LN, dtype=BF16),
         shape(LEV, 2 * LN, COLS, dtype=BF16), shape(LEV, 8, TT, SS, LN), shape(LEV, 2, KT, SS, LN)],
        [par, ensemble[:, 0], cross_mix, sea_mask],
        [vmem(LEV, KT, ROWS, LN), vmem(LEV, KT, ROWS, LN), pltpu.VMEM((KT, ROWS, LN), jnp.int32),
         pltpu.SemaphoreType.DMA((5,))],
        in_specs=[SM, HB, HB, HB],
    )
    mats = [w1, w3, k1, k3, et, lt]
    solve_out = [shape(*FIELD), shape(*FLUX), shape(NLON_DEV, 8, LN)]
    carry_out = [shape(NLAT_DEV, PK, LN), shape(2, PK, LN), shape(*EXTRA)]
    zl, phi, msg, uh, kh = call(
        first_kernel,
        [shape(*FIELD), shape(*FLUX), shape(NLON_DEV, 24, LN), shape(*HALO), shape(2, KT + 1, SS, LN)],
        [par, ul, ml, kl, north, south] + mats,
        work,
    )
    got = exchange(msg, "lon")
    out, pack, ze, ux, kx, uhx, khx = call(
        functools.partial(carry_kernel, True),
        carry_out + [shape(*EXTRA), shape(TT, SS, LN), shape(LEV, 2, SS, LN), shape(2, SS, LN)],
        [par, got, phi, lt, el],
    )
    for step in range(2):
        got = exchange(out, "lat")
        y2, yx, yh, zl, phi, msg, px = call(
            half_kernel,
            [shape(*FIELD), shape(*EXTRA), shape(*HALO)] + solve_out + [shape(*EXTRA)],
            [par, got, pack, zl, ze, ul, ux, uh, uhx, ml, el] + mats,
            carries + [diffs] + work,
        )
        got = exchange(msg, "lon")
        out, pack, ze = call(functools.partial(carry_kernel, False), carry_out, [par, got, phi, px, lt, el])
        got = exchange(out, "lat")
        if step == 1:
            break
        ul, ux, uh, uhx, zl, phi, msg, px = call(
            step_kernel,
            [shape(*FIELD), shape(*EXTRA), shape(*HALO), shape(LEV, 2, SS, LN)] + solve_out + [shape(*EXTRA)],
            [par, got, pack, zl, ze, y2, yx, yh, kl, kx, kh, khx, ml, el] + mats,
            carries + [vmem(*HALO), diffs] + work,
        )
        got = exchange(msg, "lon")
        out, pack, ze = call(functools.partial(carry_kernel, False), carry_out, [par, got, phi, px, lt, el])
    (final,) = call(
        last_kernel,
        [shape(LEV, ROWS, COLS)],
        [par, got, pack, zl, ze, y2, kl, el, lt],
        carries + [vmem(LEV, KT, ROWS, LN), pltpu.SemaphoreType.DMA((LEV,))],
        out_specs=[HB],
    )
    return final[:, None]


def solution(mesh):
    in_specs = (
        P(None, None, "lat", "lon"),
        P(None, "lat", "lon"),
        P("lat", "lon"),
        P(),
        P(),
        P(),
        P(),
    )
    out_specs = P(None, None, "lat", "lon")
    return jax.shard_map(shards, mesh=mesh, in_specs=in_specs, out_specs=out_specs, check_vma=False)
```

time: 1270 us -> 197 us (0.16)
  local copies, waits for them, and re-layouts: 524 us -> 6.15 us
  blocking collectives: 441 us -> 92.5 us
  other arithmetic: 130 us -> 1.51 us
  Pallas kernels: 0 us -> 91.6 us
  waiting for transfers between devices: 79.7 us -> 0.01 us
  starting transfers between devices: 51.2 us -> 4.6 us
  matrix products: 31.6 us -> 0 us
    all_to_all x14 -> x8, blocking collectives: 441 us -> 92.5 us  [exchange(): return lax.all_to_all(values, axis, split_axis=0, concat_axis=0, tiled=True)]
    unnamed x34 -> x18, local copies, waits for them, and re-layouts: 236 us -> 4.28 us
    all_to_all x25 -> x0, local copies, waits for them, and re-layouts: 141 us -> none  [the longest x5 86.9 us: lon_lines_solve(): lax.all_to_all(finished, 'lon', split_axis=3, concat_axis=2, tiled=True)]
    pallas_call x0 -> x10, Pallas kernels: none -> 91.6 us  [call(): pl.pallas_call(kernel, out_shape=outs, in_specs=in_specs or [SM] + [VM] *...]
    reshape x8 -> x1, local copies, waits for them, and re-layouts: 87.8 us -> 0.08 us  [parameters(): jnp.stack([theta[0], theta[1], a[0], a[1], scale[0], scale[1], zero, zero...]
    sub x10 -> x0, other arithmetic: 72.6 us -> none  [the longest x2 26.6 us: shards(): first_lon = solve_lon(start_value - scale_lon * along_lon)]
    all_to_all x2 -> x0, waiting for transfers between devices: 54.5 us -> none  [the longest x1 28.4 us: lat_lines_solve(): lax.all_to_all(values, 'lat', split_axis=3, concat_axis=2, tiled=True)]
    all_to_all x4 -> x0, other arithmetic: 33.9 us -> none  [lon_lines_solve(): lax.all_to_all(finished, 'lon', split_axis=3, concat_axis=2, tiled=True)]
  transfers between devices with their start and end apart: 18 -> 2, of which waited for: 13 -> 0; matrix products, arithmetic and copies ran while one was open for 0% -> 0% of each run, Pallas kernels for 0% -> 3%
where the time goes in v1:
time: 197 us; the launch traced here: 196 us
  blocking collectives  92.5 us (47%)
  Pallas kernels  91.6 us (46%)
  local copies, waits for them, and re-layouts  6.15 us (3%)
  starting transfers between devices  4.6 us (2%)
    all_to_all x8, blocking collectives, exchange(): return lax.all_to_all(values, axis, split_axis=0, concat_axis=0, tiled=True)  92.5 us
    pallas_call x10, Pallas kernels, call(): pl.pallas_call(kernel, out_shape=outs, in_specs=in_specs or [SM] + [VM] *...  91.6 us
    unnamed x18, local copies, waits for them, and re-layouts  4.28 us
  transfers between devices with their start and end apart: 2, of which 0 were waited for; matrix products, arithmetic and copies ran while one was open for 0% of the time, Pallas kernels for 3%

profile of v1, /device:TPU:1, one launch (start us, length us, event | category | flops | bytes accessed | tf_op | source)
XLA Modules:
  0.0 196.5 jit_solution(10523153098320073991)
XLA Ops:
  0.0 1.1 fusion.2
  1.1 1.3 convert_element_type.7
  2.5 1.5 collective-permute-start.1
  4.0 3.1 %collective-permute-start = (f32[3,16,128]{2,1,0:T(8,128)S(1)}, f32[3,16,128]{2,1,0:T(8,128)S(1)}, u32[]{:S(2)}, u32[]{:S(2)}) collective-permute-start(f32[3,16,128]{2,1,0:T(8,128)S(1)} %get-tuple-element.114), channel_id=1, source_target_pairs={{8,16},{24,32},{40,48},{56,64},{72,80},{88,96},{104,112},{16,8},{3... | collective-permute-start | bytes 73736 | tf_op jit(solution)/shard_map/ppermute | solution.py:606
  8.0 5.3 %shard_map.46 = (f32[2,16,16,8,128]{4,3,2,1,0:T(8,128)S(1)}, f32[2,16,16,8,128]{4,3,2,1,0:T(8,128)S(1)}, f32[16,16,8,128]{3,2,1,0:T(8,128)S(1)}, bf16[2,16,128,2...) custom-call(f32[18]{0:T(128)S(1)} %pad_maximum_fusion.2.par.refs_0_,, ...), custom_call_target="tpu_custom_call" | custom-call | tf_op jit(solution)/shard_map/pallas_call | solution.py:583
  13.4 1.3 copy-done.2
  14.7 17.5 %shard_map.47 = (f32[2,16,16,8,128]{4,3,2,1,0:T(8,128)S(1)}, f32[2,2,16,8,128]{4,3,2,1,0:T(8,128)S(1)}, f32[8,24,128]{2,1,0:T(8,128)S(1)}, f32[2,2,17,8,128]{4,3,2,1,0:T(8,128)S(1)}, f32[2,17,8,128]{3,2,1,0:T(8,128)S(1)}) custom-call(f32[18]{0:T(128)S(1)} %pad_maximum_fusion.2.par.refs_0_, f32[2,16,16,8,128]{4,3,2,1,0:T(8,128)S(1)} %get-tuple-element.56.ul, ...), custom_call_target="tpu_custom_call" | custom-call | tf_op jit(solution)/shard_map/pallas_call | solution.py:583
  32.2 11.1 %all_to_all.40.refs_1_ = f32[8,24,128]{2,1,0:T(8,128)S(1)} all-to-all(f32[8,24,128]{2,1,0:T(8,128)S(1)} %get-tuple-element.65), channel_id=1, replica_groups=mesh['lat'=16,'lon'=8] {'lon'}, dimensions={0} | all-to-all | bytes 196608 | tf_op jit(solution)/shard_map/all_to_all | solution.py:622
  43.4 1.1 shard_map.48
  44.4 17.0 %all_to_all.41.got = f32[16,40,128]{2,1,0:T(8,128)S(1)} all-to-all(f32[16,40,128]{2,1,0:T(8,128)S(1)} %get-tuple-element.68), channel_id=1, replica_groups=mesh['lat'=16,'lon'=8] {'lat'}, dimensions={0} | all-to-all | bytes 655360 | tf_op jit(solution)/shard_map/all_to_all | solution.py:622
  61.4 19.1 %shard_map.49 = (f32[2,16,16,8,128]{4,3,2,1,0:T(8,128)S(1)}, f32[2,16,8,128]{3,2,1,0:T(8,128)S(1)}, f32[2,2,17,8,128]{4,3,2,1,0:T(8,128)S(1)}, f32[2,16,16,8,128...) custom-call(f32[18]{0:T(128)S(1)} %pad_maximum_fusion.2.par.refs_0_,, ...), custom_call_target="tpu_custom_call" | custom-call | tf_op jit(solution)/shard_map/pallas_call | solution.py:583
  80.5 1.4 copy-done.6
  81.8 7.7 %all_to_all.42.refs_1_ = f32[8,8,128]{2,1,0:T(8,128)S(1)} all-to-all(f32[8,8,128]{2,1,0:T(8,128)S(1)} %get-tuple-element.75), channel_id=1, replica_groups=mesh['lat'=16,'lon'=8] {'lon'}, dimensions={0} | all-to-all | bytes 65536 | tf_op jit(solution)/shard_map/all_to_all | solution.py:622
  89.6 0.9 shard_map.50
  90.5 13.8 %all_to_all.43.got = f32[16,40,128]{2,1,0:T(8,128)S(1)} all-to-all(f32[16,40,128]{2,1,0:T(8,128)S(1)} %get-tuple-element.78), channel_id=1, replica_groups=mesh['lat'=16,'lon'=8] {'lat'}, dimensions={0} | all-to-all | bytes 655360 | tf_op jit(solution)/shard_map/all_to_all | solution.py:622
  104.3 1.6 copy-done.5
  105.9 20.8 %shard_map.51 = (f32[2,16,16,8,128]{4,3,2,1,0:T(8,128)S(1)}, f32[2,16,8,128]{3,2,1,0:T(8,128)S(1)}, f32[2,2,17,8,128]{4,3,2,1,0:T(8,128)S(1)}, f32[2,2,8,128]{3,...) custom-call(f32[18]{0:T(128)S(1)} %pad_maximum_fusion.2.par.refs_0_,, ...), custom_call_target="tpu_custom_call" | custom-call | tf_op jit(solution)/shard_map/pallas_call | solution.py:583
  126.6 7.5 %all_to_all.44.refs_1_ = f32[8,8,128]{2,1,0:T(8,128)S(1)} all-to-all(f32[8,8,128]{2,1,0:T(8,128)S(1)} %get-tuple-element.88), channel_id=1, replica_groups=mesh['lat'=16,'lon'=8] {'lon'}, dimensions={0} | all-to-all | bytes 65536 | tf_op jit(solution)/shard_map/all_to_all | solution.py:622
  135.0 14.1 %all_to_all.45.got = f32[16,40,128]{2,1,0:T(8,128)S(1)} all-to-all(f32[16,40,128]{2,1,0:T(8,128)S(1)} %get-tuple-element.91), channel_id=1, replica_groups=mesh['lat'=16,'lon'=8] {'lat'}, dimensions={0} | all-to-all | bytes 655360 | tf_op jit(solution)/shard_map/all_to_all | solution.py:622
  149.1 19.7 %shard_map.53 = (f32[2,16,16,8,128]{4,3,2,1,0:T(8,128)S(1)}, f32[2,16,8,128]{3,2,1,0:T(8,128)}, f32[2,2,17,8,128]{4,3,2,1,0:T(8,128)}, f32[2,16,16,8,128]{4,3,2,...) custom-call(f32[18]{0:T(128)S(1)} %pad_maximum_fusion.2.par.refs_0_, ...), custom_call_target="tpu_custom_call" | custom-call | tf_op jit(solution)/shard_map/pallas_call | solution.py:583
  168.9 7.5 %all_to_all.46.refs_1_ = f32[8,8,128]{2,1,0:T(8,128)S(1)} all-to-all(f32[8,8,128]{2,1,0:T(8,128)S(1)} %get-tuple-element.99), channel_id=1, replica_groups=mesh['lat'=16,'lon'=8] {'lon'}, dimensions={0} | all-to-all | bytes 65536 | tf_op jit(solution)/shard_map/all_to_all | solution.py:622
  176.3 0.9 shard_map.54
  177.2 13.8 %all_to_all.47.got = f32[16,40,128]{2,1,0:T(8,128)S(1)} all-to-all(f32[16,40,128]{2,1,0:T(8,128)S(1)} %get-tuple-element.102), channel_id=1, replica_groups=mesh['lat'=16,'lon'=8] {'lat'}, dimensions={0} | all-to-all | bytes 655360 | tf_op jit(solution)/shard_map/all_to_all | solution.py:622
  191.0 5.5 %shard_map.55 = f32[2,128,2048]{2,1,0:T(8,128)} custom-call(f32[18]{0:T(128)S(1)} %pad_maximum_fusion.2.par.refs_0_, f32[16,40,128]{2,1,0:T(8,128)S(1)} %all_to_all.47.got, f32[2,40,128]{2,1,0:T(8,128)S(1)} %get-tuple-element.103.pack, f32[2,16,16,8,128]{4,3,2,1,0:T(8,128)S(1)} %get-tuple-element.104.zl, f32[2,16,8,128]{3,2,1,0:T(8,128)S(1)} %get-tuple-element.105.ze, ...), custom_call_target="tpu_custom_call" | custom-call | tf_op jit(solution)/shard_map/pallas_call | solution.py:583
  (35 shorter events, 1.9 us)
Async XLA Ops:
  0.0 8.0 %copy-start.3 = (s32[128,2048]{1,0:T(8,128)S(1)}, s32[128,2048]{1,0:T(8,128)}, u32[]{:S(2)}) copy-start(s32[128,2048]{1,0:T(8,128)} %k_hbm.1) | copy-start | bytes 3145732
  0.0 7.1 %copy-start.8 = (f32[2,2]{1,0:T(2,128)S(1)}, f32[2,2]{1,0:T(2,128)}, u32[]{:S(2)}) copy-start(f32[2,2]{1,0:T(2,128)} %param.10) | copy-start | bytes 52
  2.5 12.2 %collective-permute-start.1 = (f32[3,16,128]{2,1,0:T(8,128)S(1)}, f32[3,16,128]{2,1,0:T(8,128)S(1)}, u32[]{:S(2)}, u32[]{:S(2)}) collective-permute-start(f32[3,16,128]{2,1,0:T(8,128)S(1)} %get-tuple-element.113), channel_id=1, source_target_pairs={{0,8},{16,24},{32,40},{48,56},{64,72},{80,88},{96,104},{112,120},{... | collective-permute-start | bytes 73736 | tf_op jit(solution)/shard_map/ppermute | solution.py:605
  4.0 10.7 %collective-permute-start = (f32[3,16,128]{2,1,0:T(8,128)S(1)}, f32[3,16,128]{2,1,0:T(8,128)S(1)}, u32[]{:S(2)}, u32[]{:S(2)}) collective-permute-start(f32[3,16,128]{2,1,0:T(8,128)S(1)} %get-tuple-element.114), channel_id=1, source_target_pairs={{8,16},{24,32},{40,48},{56,64},{72,80},{88,96},{104,112},{16,8},{3... | collective-permute-start | bytes 73736 | tf_op jit(solution)/shard_map/ppermute | solution.py:606
  13.4 1.3 copy-start.2
  14.7 17.5 %copy-start = (f32[2,16,16,8,128]{4,3,2,1,0:T(8,128)}, f32[2,16,16,8,128]{4,3,2,1,0:T(8,128)S(1)}, u32[]{:S(2)}) copy-start(f32[2,16,16,8,128]{4,3,2,1,0:T(8,128)S(1)} %get-tuple-element.57.ml) | copy-start | bytes 6291460
  14.7 17.5 %copy-start.1 = (bf16[2,16,128,256]{3,2,1,0:T(8,128)(2,1)}, bf16[2,16,128,256]{3,2,1,0:T(8,128)(2,1)S(1)}, u32[]{:S(2)}) copy-start(bf16[2,16,128,256]{3,2,1,0:T(8,128)(2,1)S(1)} %get-tuple-element.59.w1) | copy-start | bytes 6291460
  80.5 1.4 copy-start.6
  81.8 22.4 %copy-start.4 = (f32[2,16,16,8,128]{4,3,2,1,0:T(8,128)}, f32[2,16,16,8,128]{4,3,2,1,0:T(8,128)S(1)}, u32[]{:S(2)}) copy-start(f32[2,16,16,8,128]{4,3,2,1,0:T(8,128)S(1)} %get-tuple-element.82.y2) | copy-start | bytes 6291460
  81.8 22.4 %copy-start.7 = (f32[2,16,16,8,128]{4,3,2,1,0:T(8,128)S(1)}, f32[2,16,16,8,128]{4,3,2,1,0:T(8,128)}, u32[]{:S(2)}) copy-start(f32[2,16,16,8,128]{4,3,2,1,0:T(8,128)} %copy-done.6) | copy-start | bytes 6291460
  104.3 1.6 copy-start.5

commit v2 on v1

--- a/solution.py
+++ b/solution.py
@@ -14,8 +14,8 @@
 F32, BF16 = jnp.float32, jnp.bfloat16
 VM = pl.BlockSpec(memory_space=pltpu.VMEM)
 SM = pl.BlockSpec(memory_space=pltpu.SMEM)
-HB = pl.BlockSpec(memory_space=pl.ANY)
-PARAMS = pltpu.CompilerParams(vmem_limit_bytes=40 * 1024 * 1024)
+HB = pl.BlockSpec(memory_space=pltpu.HBM)
+PARAMS = pltpu.CompilerParams(vmem_limit_bytes=10 * 1024 * 1024)
 
 L_P, L_LQ, L_Q, L_CQ, L_CQL, L_CP, L_GQ, L_GP = range(8)
 PK = 40
@@ -35,11 +35,11 @@
 
 class Rates:
     def __init__(self, par, level):
-        self.t1, self.t2, self.a1, self.a2, self.c1, self.c2 = (par[8 * level + i] for i in range(6))
+        self.t1, self.t2, self.a1, self.a2, self.c1, self.c2 = (par[2 * i + level] for i in range(6))
 
 
 def position(par):
-    return par[16], par[17]
+    return par[12], par[13]
 
 
 def split3(x):
@@ -131,18 +131,20 @@
     lax.fori_loop(0, KT, move, 0)
 
 
-def right_left(tiles, ext):
-    lane = iota((1, SS, LN), 2)
-    right = pltpu.roll(tiles, LN - 1, 2)
-    left = pltpu.roll(tiles, 1, 2)
-    if ext is None:
-        beyond_right = before_left = jnp.zeros((1, SS, LN), F32)
-    else:
-        beyond_right = pltpu.roll(ext, LN - 2, 1)[None]
-        before_left = ext[None]
-    next_right = jnp.concatenate([right[1:], beyond_right], axis=0)
-    prev_left = jnp.concatenate([before_left, left[:-1]], axis=0)
-    return jnp.where(lane == LN - 1, next_right, right), jnp.where(lane == 0, prev_left, left)
+def turned(tiles, ext):
+    lane = iota((SS, LN), 1)
+    at_end, at_start = lane == LN - 1, lane == 0
+    zero = jnp.zeros((SS, LN), F32)
+    before = zero if ext is None else ext
+    right = pltpu.roll(tiles(0), LN - 1, 1)
+    for k in range(KT):
+        if k + 1 < KT:
+            beyond = pltpu.roll(tiles(k + 1), LN - 1, 1)
+        else:
+            beyond = zero if ext is None else pltpu.roll(ext, LN - 2, 1)
+        left = pltpu.roll(tiles(k), 1, 1)
+        yield jnp.where(at_end, beyond, right), jnp.where(at_start, before, left)
+        right, before = beyond, left
 
 
 def north_of(last, halo):
@@ -203,7 +205,9 @@
             two = dot(lhs2, jnp.concatenate([ww[:, :LN], w3[l, k]], axis=0))
             return ab + (one[:, :LN] + one[:, LN:] + two)
 
-        ab = lax.fori_loop(0, KT, tile, jnp.zeros((ROWS, LN), F32))
+        ab = jnp.zeros((ROWS, LN), F32)
+        for k in range(KT):
+            ab = tile(k, ab)
         sums.append(ab)
         high, mid, low = split3(ab)
         lane = iota((ROWS, LN), 1)
@@ -224,7 +228,9 @@
             return s, acc + lt[l, L_LQ, t] * x
 
         zero = jnp.zeros((KT, SS, LN), F32)
-        last, acc = lax.fori_loop(0, TT, down, (zero, zero))
+        last, acc = zero, zero
+        for t in range(TT):
+            last, acc = down(t, (last, acc))
         carry_down, carry_up, phi_l, psi_l = chunk_ends(last, acc, r.t2)
         phi[l, 0] = phi_l
         phi[l, 1] = psi_l
@@ -234,17 +240,26 @@
             zl[l, :, t] = lt[l, L_CQ, t] * ss[:, t] + lt[l, L_CQL, t] * carry_down + lt[l, L_CP, t] * u
             return lam * (u + lt[l, L_Q, t] * xs[l, :, t])
 
-        lax.fori_loop(0, TT, up, lam * carry_up)
+        u = lam * carry_up
+        for i in range(TT):
+            u = up(i, u)
     return sums
 
 
-def explicit(r, before, here, after, ext_here, ext_diff, mixing, mask):
-    east, west = right_left(here, ext_here)
-    lon = east + west - 2.0 * here
-    lat = after + before - 2.0 * here
-    east, west = right_left(after - before, ext_diff)
-    q = mask * (here + mixing * (east - west) + (2.0 * r.a1) * lon + (2.0 * r.a2) * lat) - r.a1 * lon
-    return q, -r.a2 * lat
+def explicit(r, l, t, before, here, after, ext_here, ext_diff, ml, kl, qs, xs):
+    here = [here(k) for k in range(KT)]
+    around = []
+    diff = []
+    for k in range(KT):
+        up, down = before(k), after(k)
+        around.append(down + up - 2.0 * here[k])
+        diff.append(down - up)
+    flat = zip(turned(lambda k: here[k], ext_here), turned(lambda k: diff[k], ext_diff))
+    for k, ((east, west), (diff_east, diff_west)) in enumerate(flat):
+        lon = east + west - 2.0 * here[k]
+        inner = here[k] + ml[l, k, t] * (diff_east - diff_west) + (2.0 * r.a1) * lon + (2.0 * r.a2) * around[k]
+        qs[l, k, t] = kl[k, t] * inner - r.a1 * lon
+        xs[l, k, t] = -r.a2 * around[k]
 
 
 def end_columns(first, last):
@@ -264,19 +279,16 @@
         uh[l, 0, :KT] = spread(north, l)
         uh[l, 1, :KT] = spread(south, l)
 
-        def rows(t, before, after):
-            q, p = explicit(r, before, ul[l, :, t], after, None, None, ml[l, :, t], kl[:, t])
-            qs[l, :, t] = q
-            xs[l, :, t] = p
-
-        rows(0, north_of(ul[l, :, TT - 1], uh[l, 0, :KT]), ul[l, :, 1])
-
-        def body(t, carry):
-            rows(t, ul[l, :, t - 1], ul[l, :, t + 1])
-            return carry
-
-        lax.fori_loop(1, TT - 1, body, 0)
-        rows(TT - 1, ul[l, :, TT - 2], south_of(ul[l, :, 0], uh[l, 1, :KT]))
+        for t in range(TT):
+            if t == 0:
+                before = lambda k: north_of(ul[l, k, TT - 1], uh[l, 0, k])
+            else:
+                before = lambda k, t=t: ul[l, k, t - 1]
+            if t == TT - 1:
+                after = lambda k: south_of(ul[l, k, 0], uh[l, 1, k])
+            else:
+                after = lambda k, t=t: ul[l, k, t + 1]
+            explicit(r, l, t, before, lambda k, t=t: ul[l, k, t], after, None, None, ml, kl, qs, xs)
     sums = local_solve(par, qs, xs, ss, w1, w3, k1, k3, et, lt, zl, phi, True)
     parts = []
     for l in range(LEV):
@@ -470,13 +482,23 @@
                 hb[l, 1, k] = wide(south)
 
 
-def solved_rows(l, t, zl, ze, el, lt, tb, vb):
-    extra = ze[l, t]
-    gq, gp = lt[l, L_GQ, t], lt[l, L_GP, t]
-    z_left = jnp.broadcast_to(extra[:, 2:3], (SS, LN))
-    z_right = jnp.broadcast_to(extra[:, 3:4], (SS, LN))
-    own = zl[l, :, t] + el[l, 0] * z_left + el[l, 1] * z_right + gq * tb[l, :KT] + gp * vb[l, :KT]
-    return own, extra + gq * tb[l, KT] + gp * vb[l, KT]
+def solved_rows(l, zl, ze, el, lt, tb, vb, use, use_extra):
+    step = 4
+    for start in range(0, TT, step):
+        times = range(start, start + step)
+        extra = [ze[l, t] for t in times]
+        gq = [lt[l, L_GQ, t] for t in times]
+        gp = [lt[l, L_GP, t] for t in times]
+        z_left = [jnp.broadcast_to(x[:, 2:3], (SS, LN)) for x in extra]
+        z_right = [jnp.broadcast_to(x[:, 3:4], (SS, LN)) for x in extra]
+        for k in range(KT):
+            e_left, e_right, above, below = el[l, 0, k], el[l, 1, k], tb[l, k], vb[l, k]
+            for i, t in enumerate(times):
+                use(k, t, zl[l, k, t] + e_left * z_left[i] + e_right * z_right[i] + gq[i] * above + gp[i] * below)
+        if use_extra is not None:
+            above, below = tb[l, KT], vb[l, KT]
+            for i, t in enumerate(times):
+                use_extra(t, extra[i] + gq[i] * above + gp[i] * below)
 
 
 def send_sums(sums, msg):
@@ -491,27 +513,24 @@
     for l in range(LEV):
         r = Rates(par, l)
 
-        def rows(t, carry):
-            own, extra = solved_rows(l, t, zl, ze, el, lt, tb, vb)
-            y2[l, :, t] = own
+        def use(k, t, own):
+            y2[l, k, t] = own
+            vs[k, t + 1] = own - ul[l, k, t]
+
+        def use_extra(t, extra):
             yx[l, t] = extra
-            vs[:KT, t + 1] = own - ul[l, :, t]
             vs[KT, t + 1] = extra - ux[l, t]
             px[l, t] = jnp.zeros((SS, LN), F32)
-            return carry
-
-        lax.fori_loop(0, TT, rows, 0)
+
+        solved_rows(l, zl, ze, el, lt, tb, vb, use, use_extra)
         for side, edge, at, turn in ((0, TT, 0, north_of), (1, 1, TT + 1, south_of)):
             vs[:KT, at] = turn(vs[:KT, edge], yh[l, side, :KT] - uh[l, side, :KT])
             vs[KT, at] = turn(vs[KT, edge], yh[l, side, KT] - uhx[l, side])
 
-        def body(t, carry):
-            diff = vs[:, t + 2] - vs[:, t]
-            east, west = right_left(diff[:KT], diff[KT])
-            qs[l, :, t] = 0.5 * ml[l, :, t] * (east - west)
-            return carry
-
-        lax.fori_loop(0, TT, body, 0)
+        for t in range(TT):
+            diff = [vs[k, t + 2] - vs[k, t] for k in range(KT + 1)]
+            for k, (east, west) in enumerate(turned(lambda k: diff[k], diff[KT])):
+                qs[l, k, t] = 0.5 * ml[l, k, t] * (east - west)
     send_sums(local_solve(par, qs, xs, ss, w1, w3, k1, k3, et, lt, zo, phi, False), msg)
 
 
@@ -521,17 +540,17 @@
     for l in range(LEV):
         r = Rates(par, l)
 
-        def rows(t, carry):
-            own, extra = solved_rows(l, t, zl, ze, el, lt, tb, vb)
-            own = kl[:, t] * (own + y2[l, :, t])
+        def use(k, t, own):
+            own = kl[k, t] * (own + y2[l, k, t])
+            un[l, k, t] = own
+            vs[k, t + 1] = own
+
+        def use_extra(t, extra):
             extra = kx[t] * (extra + yx[l, t])
-            un[l, :, t] = own
             unx[l, t] = extra
-            vs[:KT, t + 1] = own
             vs[KT, t + 1] = extra
-            return carry
-
-        lax.fori_loop(0, TT, rows, 0)
+
+        solved_rows(l, zl, ze, el, lt, tb, vb, use, use_extra)
         for side, edge, at, turn in ((0, TT, 0, north_of), (1, 1, TT + 1, south_of)):
             halo = kh[side, :KT] * (yh[l, side, :KT] + hb[l, side, :KT])
             halo_x = khx[side] * (yh[l, side, KT] + hb[l, side, KT])
@@ -540,16 +559,11 @@
             vs[:KT, at] = turn(vs[:KT, edge], halo)
             vs[KT, at] = turn(vs[KT, edge], halo_x)
 
-        def body(t, carry):
-            before, here, after = vs[:, t], vs[:, t + 1], vs[:, t + 2]
-            q, p = explicit(r, before[:KT], here[:KT], after[:KT], here[KT], (after - before)[KT], ml[l, :, t], kl[:, t])
-            qs[l, :, t] = q
-            xs[l, :, t] = p
-            extra = -r.a2 * (after[KT] + before[KT] - 2.0 * here[KT])
-            px[l, t] = jnp.where(iota((SS, LN), 1) < 2, extra, 0.0)
-            return carry
-
-        lax.fori_loop(0, TT, body, 0)
+        for t in range(TT):
+            before, here, after = vs[KT, t], vs[KT, t + 1], vs[KT, t + 2]
+            explicit(r, l, t, lambda k: vs[k, t], lambda k: vs[k, t + 1], lambda k: vs[k, t + 2],
+                     here, after - before, ml, kl, qs, xs)
+            px[l, t] = jnp.where(iota((SS, LN), 1) < 2, -r.a2 * (after + before - 2.0 * here), 0.0)
     send_sums(local_solve(par, qs, xs, ss, w1, w3, k1, k3, et, lt, zo, phi, True), msg)
 
 
@@ -558,14 +572,10 @@
     copies = []
     for l in range(LEV):
 
-        def rows(t, carry):
-            own, _ = solved_rows(l, t, zl, ze, el, lt, tb, vb)
-            own = kl[:, t] * (own + y2[l, :, t])
-            for k in range(KT):
-                os[l, k, pl.ds(t, SS, stride=TT), :] = own[k]
-            return carry
-
-        lax.fori_loop(0, TT, rows, 0)
+        def use(k, t, own):
+            os[l, k, pl.ds(t, SS, stride=TT), :] = kl[k, t] * (own + y2[l, k, t])
+
+        solved_rows(l, zl, ze, el, lt, tb, vb, use, None)
         for k in range(KT):
             copies.append(pltpu.make_async_copy(os.at[l, k], out.at[l, :, pl.ds(k * LN, LN)], sem.at[l]))
             copies[-1].start()
@@ -596,8 +606,8 @@
 
 def halo_rows(ensemble, mask):
     at = lax.axis_index("lat")
-    first = jnp.concatenate([ensemble[:, 0, 0, :], mask[0:1, :]], axis=0).reshape(3, KT, LN)
-    last = jnp.concatenate([ensemble[:, 0, ROWS - 1, :], mask[ROWS - 1 :, :]], axis=0).reshape(3, KT, LN)
+    first = jnp.concatenate([ensemble[:, 0, 0, :], mask[0:1, :].astype(F32)], axis=0).reshape(3, KT, LN)
+    last = jnp.concatenate([ensemble[:, 0, ROWS - 1, :], mask[ROWS - 1 :, :].astype(F32)], axis=0).reshape(3, KT, LN)
     even = at % 2 == 0
     pairs = [(i, i + 1) for i in range(0, NLAT_DEV, 2)]
     odd_pairs = [(i, i + 1) for i in range(1, NLAT_DEV - 1, 2)]
@@ -612,10 +622,8 @@
     half = 0.5 / jnp.sqrt(a)
     theta = 2.0 * jnp.log1p(half + half * half / (1.0 + jnp.sqrt(1.0 + half * half)))
     scale = 1.0 / jnp.sqrt(1.0 + 4.0 * a)
-    zero = jnp.zeros((LEV,), F32)
-    table = jnp.stack([theta[0], theta[1], a[0], a[1], scale[0], scale[1], zero, zero], axis=1).reshape(-1)
     where = jnp.stack([lax.axis_index("lat"), lax.axis_index("lon")]).astype(F32)
-    return jnp.concatenate([table, where])
+    return jnp.concatenate([jnp.stack([theta, a, scale]).reshape(-1), where])
 
 
 def exchange(values, axis):
@@ -624,7 +632,7 @@
 
 def shards(ensemble, cross_mix, sea_mask, level_rates, panel_inverse, reduced_lon, reduced_lat):
     par = parameters(level_rates)
-    north, south = halo_rows(ensemble, sea_mask.astype(F32))
+    north, south = halo_rows(ensemble, sea_mask)
     work = [vmem(*FIELD), vmem(*FIELD), vmem(KT, TT, SS, LN)]
     carries = [vmem(LEV, KT + 1, SS, LN), vmem(LEV, KT + 1, SS, LN)]
     diffs = vmem(KT + 1, TT + 2, SS, LN)

time: 197 us -> 145 us (0.74)
  Pallas kernels: 91.6 us -> 38.6 us
    pallas_call x10, Pallas kernels: 91.6 us -> 38.6 us  [call(): pl.pallas_call(kernel, out_shape=outs, in_specs=in_specs or [SM] + [VM] *...]
    unnamed x18 -> x6, local copies, waits for them, and re-layouts: 4.28 us -> 4.41 us
  transfers between devices with their start and end apart: 2 -> 2, of which waited for: 0 -> 0; matrix products, arithmetic and copies ran while one was open for 0% -> 1% of each run, Pallas kernels for 3% -> 4%
where the time goes in v2:
time: 145 us; the launch traced here: 144 us
  blocking collectives  92.5 us (64%)
  Pallas kernels  38.6 us (27%)
  local copies, waits for them, and re-layouts  5.49 us (4%)
  starting transfers between devices  4.6 us (3%)
  other arithmetic  2.46 us (2%)
    all_to_all x8, blocking collectives, exchange(): return lax.all_to_all(values, axis, split_axis=0, concat_axis=0, tiled=True)  92.5 us
    pallas_call x10, Pallas kernels, call(): pl.pallas_call(kernel, out_shape=outs, in_specs=in_specs or [SM] + [VM] *...  38.6 us
    unnamed x6, local copies, waits for them, and re-layouts  4.41 us
    ppermute x1, starting transfers between devices, halo_rows(): two = lax.ppermute(jnp.where(even, first, last), 'lat', both(odd_pairs))  3.1 us
  transfers between devices with their start and end apart: 2, of which 0 were waited for; matrix products, arithmetic and copies ran while one was open for 1% of the time, Pallas kernels for 4%

profile of v2, /device:TPU:1, one launch (start us, length us, event | category | flops | bytes accessed | tf_op | source)
XLA Modules:
  0.0 143.9 jit_solution(4983061299978346729)
XLA Ops:
  0.0 0.9 slice_convert_fusion.1
  0.9 1.0 fusion.2
  1.9 1.5 %collective-permute-start.1 = (f32[3,16,128]{2,1,0:T(8,128)S(1)}, f32[3,16,128]{2,1,0:T(8,128)S(1)}, u32[]{:S(2)}, u32[]{:S(2)}) collective-permute-start(f32[3,16,128]{2,1,0:T(8,128)S(1)} %get-tuple-element.113), channel_id=1, source_target_pairs={{0,8},{16,24},{32,40},{48,56},{64,72},{80,88},{96,104},{112,120},{... | collective-permute-start | bytes 73736 | tf_op jit(solution)/shard_map/ppermute | solution.py:615
  3.4 3.1 %collective-permute-start = (f32[3,16,128]{2,1,0:T(8,128)S(1)}, f32[3,16,128]{2,1,0:T(8,128)S(1)}, u32[]{:S(2)}, u32[]{:S(2)}) collective-permute-start(f32[3,16,128]{2,1,0:T(8,128)S(1)} %get-tuple-element.114), channel_id=1, source_target_pairs={{8,16},{24,32},{40,48},{56,64},{72,80},{88,96},{104,112},{16,8},{3... | collective-permute-start | bytes 73736 | tf_op jit(solution)/shard_map/ppermute | solution.py:616
  8.2 1.6 %copy-done = f32[2,1,128,2048]{3,2,1,0:T(8,128)S(1)} copy-done((f32[2,1,128,2048]{3,2,1,0:T(8,128)S(1)}, f32[2,1,128,2048]{3,2,1,0:T(8,128)}, u32[]{:S(2)}) %copy-start) | copy-done | bytes 2097176
  9.8 1.6 %copy-done.1 = f32[2,128,2048]{2,1,0:T(8,128)S(1)} copy-done((f32[2,128,2048]{2,1,0:T(8,128)S(1)}, f32[2,128,2048]{2,1,0:T(8,128)}, u32[]{:S(2)}) %copy-start.1) | copy-done | bytes 2097176
  11.3 1.2 copy-done.2
  12.6 5.9 %shard_map.46 = (f32[2,16,16,8,128]{4,3,2,1,0:T(8,128)S(1)}, f32[2,16,16,8,128]{4,3,2,1,0:T(8,128)S(1)}, f32[16,16,8,128]{3,2,1,0:T(8,128)S(1)}, bf16[2,16,128,2...) custom-call(f32[14]{0:T(128)S(1)} %pad_maximum_fusion.3.par.refs_0_,, ...), custom_call_target="tpu_custom_call" | custom-call | tf_op jit(solution)/shard_map/pallas_call | solution.py:593
  18.5 6.4 %shard_map.47 = (f32[2,16,16,8,128]{4,3,2,1,0:T(8,128)S(1)}, f32[2,2,16,8,128]{4,3,2,1,0:T(8,128)S(1)}, f32[8,24,128]{2,1,0:T(8,128)S(1)}, f32[2,2,17,8,128]{4,3,2,1,0:T(8,128)S(1)}, f32[2,17,8,128]{3,2,1,0:T(8,128)S(1)}) custom-call(f32[14]{0:T(128)S(1)} %pad_maximum_fusion.3.par.refs_0_, f32[2,16,16,8,128]{4,3,2,1,0:T(8,128)S(1)} %get-tuple-element.56.ul, ...), custom_call_target="tpu_custom_call" | custom-call | tf_op jit(solution)/shard_map/pallas_call | solution.py:593
  24.8 11.1 %all_to_all.40.refs_1_ = f32[8,24,128]{2,1,0:T(8,128)S(1)} all-to-all(f32[8,24,128]{2,1,0:T(8,128)S(1)} %get-tuple-element.65), channel_id=1, replica_groups=mesh['lat'=16,'lon'=8] {'lon'}, dimensions={0} | all-to-all | bytes 196608 | tf_op jit(solution)/shard_map/all_to_all | solution.py:630
  36.0 1.1 shard_map.48
  37.0 17.0 %all_to_all.41.got = f32[16,40,128]{2,1,0:T(8,128)S(1)} all-to-all(f32[16,40,128]{2,1,0:T(8,128)S(1)} %get-tuple-element.68), channel_id=1, replica_groups=mesh['lat'=16,'lon'=8] {'lat'}, dimensions={0} | all-to-all | bytes 655360 | tf_op jit(solution)/shard_map/all_to_all | solution.py:630
  54.0 5.9 %shard_map.49 = (f32[2,16,16,8,128]{4,3,2,1,0:T(8,128)S(1)}, f32[2,16,8,128]{3,2,1,0:T(8,128)S(1)}, f32[2,2,17,8,128]{4,3,2,1,0:T(8,128)S(1)}, f32[2,16,16,8,128...) custom-call(f32[14]{0:T(128)S(1)} %pad_maximum_fusion.3.par.refs_0_,, ...), custom_call_target="tpu_custom_call" | custom-call | tf_op jit(solution)/shard_map/pallas_call | solution.py:593
  59.9 7.5 %all_to_all.42.refs_1_ = f32[8,8,128]{2,1,0:T(8,128)S(1)} all-to-all(f32[8,8,128]{2,1,0:T(8,128)S(1)} %get-tuple-element.75), channel_id=1, replica_groups=mesh['lat'=16,'lon'=8] {'lon'}, dimensions={0} | all-to-all | bytes 65536 | tf_op jit(solution)/shard_map/all_to_all | solution.py:630
  68.3 13.8 %all_to_all.43.got = f32[16,40,128]{2,1,0:T(8,128)S(1)} all-to-all(f32[16,40,128]{2,1,0:T(8,128)S(1)} %get-tuple-element.78), channel_id=1, replica_groups=mesh['lat'=16,'lon'=8] {'lat'}, dimensions={0} | all-to-all | bytes 655360 | tf_op jit(solution)/shard_map/all_to_all | solution.py:630
  82.1 7.7 %shard_map.51 = (f32[2,16,16,8,128]{4,3,2,1,0:T(8,128)S(1)}, f32[2,16,8,128]{3,2,1,0:T(8,128)S(1)}, f32[2,2,17,8,128]{4,3,2,1,0:T(8,128)S(1)}, f32[2,2,8,128]{3,...) custom-call(f32[14]{0:T(128)S(1)} %pad_maximum_fusion.3.par.refs_0_,, ...), custom_call_target="tpu_custom_call" | custom-call | tf_op jit(solution)/shard_map/pallas_call | solution.py:593
  89.8 7.5 %all_to_all.44.refs_1_ = f32[8,8,128]{2,1,0:T(8,128)S(1)} all-to-all(f32[8,8,128]{2,1,0:T(8,128)S(1)} %get-tuple-element.88), channel_id=1, replica_groups=mesh['lat'=16,'lon'=8] {'lon'}, dimensions={0} | all-to-all | bytes 65536 | tf_op jit(solution)/shard_map/all_to_all | solution.py:630
  97.3 0.9 shard_map.52
  98.2 14.1 %all_to_all.45.got = f32[16,40,128]{2,1,0:T(8,128)S(1)} all-to-all(f32[16,40,128]{2,1,0:T(8,128)S(1)} %get-tuple-element.91), channel_id=1, replica_groups=mesh['lat'=16,'lon'=8] {'lat'}, dimensions={0} | all-to-all | bytes 655360 | tf_op jit(solution)/shard_map/all_to_all | solution.py:630
  112.3 5.9 %shard_map.53 = (f32[2,16,16,8,128]{4,3,2,1,0:T(8,128)S(1)}, f32[2,16,8,128]{3,2,1,0:T(8,128)}, f32[2,2,17,8,128]{4,3,2,1,0:T(8,128)}, f32[2,16,16,8,128]{4,3,2,...) custom-call(f32[14]{0:T(128)S(1)} %pad_maximum_fusion.3.par.refs_0_, ...), custom_call_target="tpu_custom_call" | custom-call | tf_op jit(solution)/shard_map/pallas_call | solution.py:593
  118.2 7.5 %all_to_all.46.refs_1_ = f32[8,8,128]{2,1,0:T(8,128)S(1)} all-to-all(f32[8,8,128]{2,1,0:T(8,128)S(1)} %get-tuple-element.99), channel_id=1, replica_groups=mesh['lat'=16,'lon'=8] {'lon'}, dimensions={0} | all-to-all | bytes 65536 | tf_op jit(solution)/shard_map/all_to_all | solution.py:630
  125.7 0.9 shard_map.54
  126.5 14.0 %all_to_all.47.got = f32[16,40,128]{2,1,0:T(8,128)S(1)} all-to-all(f32[16,40,128]{2,1,0:T(8,128)S(1)} %get-tuple-element.102), channel_id=1, replica_groups=mesh['lat'=16,'lon'=8] {'lat'}, dimensions={0} | all-to-all | bytes 655360 | tf_op jit(solution)/shard_map/all_to_all | solution.py:630
  140.6 3.2 %shard_map.55 = f32[2,128,2048]{2,1,0:T(8,128)} custom-call(f32[14]{0:T(128)S(1)} %pad_maximum_fusion.3.par.refs_0_, f32[16,40,128]{2,1,0:T(8,128)S(1)} %all_to_all.47.got, f32[2,40,128]{2,1,0:T(8,128)S(1)} %get-tuple-element.103.pack, f32[2,16,16,8,128]{4,3,2,1,0:T(8,128)S(1)} %get-tuple-element.104.zl, f32[2,16,8,128]{3,2,1,0:T(8,128)S(1)} %get-tuple-element.105.ze, ...), custom_call_target="tpu_custom_call" | custom-call | tf_op jit(solution)/shard_map/pallas_call | solution.py:593
  (13 shorter events, 2.5 us)
Async XLA Ops:
  1.9 16.5 %collective-permute-start.1 = (f32[3,16,128]{2,1,0:T(8,128)S(1)}, f32[3,16,128]{2,1,0:T(8,128)S(1)}, u32[]{:S(2)}, u32[]{:S(2)}) collective-permute-start(f32[3,16,128]{2,1,0:T(8,128)S(1)} %get-tuple-element.113), channel_id=1, source_target_pairs={{0,8},{16,24},{32,40},{48,56},{64,72},{80,88},{96,104},{112,120},{... | collective-permute-start | bytes 73736 | tf_op jit(solution)/shard_map/ppermute | solution.py:615
  3.4 15.0 %collective-permute-start = (f32[3,16,128]{2,1,0:T(8,128)S(1)}, f32[3,16,128]{2,1,0:T(8,128)S(1)}, u32[]{:S(2)}, u32[]{:S(2)}) collective-permute-start(f32[3,16,128]{2,1,0:T(8,128)S(1)} %get-tuple-element.114), channel_id=1, source_target_pairs={{8,16},{24,32},{40,48},{56,64},{72,80},{88,96},{104,112},{16,8},{3... | collective-permute-start | bytes 73736 | tf_op jit(solution)/shard_map/ppermute | solution.py:616
  8.2 1.6 %copy-start = (f32[2,1,128,2048]{3,2,1,0:T(8,128)S(1)}, f32[2,1,128,2048]{3,2,1,0:T(8,128)}, u32[]{:S(2)}) copy-start(f32[2,1,128,2048]{3,2,1,0:T(8,128)} %param.7) | copy-start | bytes 6291460
  9.7 1.6 %copy-start.1 = (f32[2,128,2048]{2,1,0:T(8,128)S(1)}, f32[2,128,2048]{2,1,0:T(8,128)}, u32[]{:S(2)}) copy-start(f32[2,128,2048]{2,1,0:T(8,128)} %m_hbm.1) | copy-start | bytes 6291460
  11.3 1.2 copy-start.2

commit v3 on v2

--- a/solution.py
+++ b/solution.py
@@ -15,7 +15,6 @@
 VM = pl.BlockSpec(memory_space=pltpu.VMEM)
 SM = pl.BlockSpec(memory_space=pltpu.SMEM)
 HB = pl.BlockSpec(memory_space=pltpu.HBM)
-PARAMS = pltpu.CompilerParams(vmem_limit_bytes=10 * 1024 * 1024)
 
 L_P, L_LQ, L_Q, L_CQ, L_CQL, L_CP, L_GQ, L_GP = range(8)
 PK = 40
@@ -35,11 +34,19 @@
 
 class Rates:
     def __init__(self, par, level):
-        self.t1, self.t2, self.a1, self.a2, self.c1, self.c2 = (par[2 * i + level] for i in range(6))
-
-
-def position(par):
-    return par[12], par[13]
+        self.a1, self.a2 = par[0, level], par[1, level]
+        self.t1, self.c1 = self.decay(self.a1)
+        self.t2, self.c2 = self.decay(self.a2)
+
+    def decay(self, a):
+        a = jnp.full((1, LN), 1.0, F32) * a
+        half = 0.5 / jnp.sqrt(a)
+        theta = 2.0 * jnp.log1p(half + half * half / (1.0 + jnp.sqrt(1.0 + half * half)))
+        return theta, 1.0 / jnp.sqrt(1.0 + 4.0 * a)
+
+
+def position():
+    return lax.axis_index("lat").astype(F32), lax.axis_index("lon").astype(F32)
 
 
 def split3(x):
@@ -53,40 +60,28 @@
     return jnp.dot(x, y, preferred_element_type=F32)
 
 
-def tables_kernel(par, u_hbm, m_hbm, k_hbm, ul, ml, kl, w1, w3, k1, k3, et, lt, el, su, sm, sk, sem):
-    copies = []
-    for l in range(LEV):
-        copies.append([pltpu.make_async_copy(u_hbm.at[l, :, pl.ds(k * LN, LN)], su.at[l, k], sem.at[l]) for k in range(KT)])
-    for l in range(LEV):
-        copies.append([pltpu.make_async_copy(m_hbm.at[l, :, pl.ds(k * LN, LN)], sm.at[l, k], sem.at[2 + l]) for k in range(KT)])
-    copies.append([pltpu.make_async_copy(k_hbm.at[:, pl.ds(k * LN, LN)], sk.at[k], sem.at[4]) for k in range(KT)])
-    for group in copies:
-        for c in group:
-            c.start()
-    i_pos, _ = position(par)
+def tables_kernel(par, after, wt, kt, et, lt, el):
+    i_pos, _ = position()
     for l in range(LEV):
         r = Rates(par, l)
         dist = jnp.abs(fiota((LN, LN), 0) - fiota((LN, LN), 1))
-        high, mid, low = split3(r.c1 * jnp.exp(-r.t1 * dist))
-        k1[l] = jnp.concatenate([high, mid], axis=1)
-        k3[l] = low
+        for i, piece in enumerate(split3(r.c1 * jnp.exp(-r.t1 * dist))):
+            kt[l, i] = piece
         lane = iota((LN, LN), 1)
         row = fiota((LN, LN), 0)
         slot = lane % 32
         rising = ((lane < 96) & (slot >= 16)) | (lane == 97)
         base = jnp.exp(-r.t1 * jnp.where(rising, row, (LN - 1) - row))
 
-        def weights(k, carry):
-            kf = k.astype(F32)
+        def weights(k):
             pick = jnp.where((lane < 96) & (slot % 16 == k), 1.0, 0.0)
-            pick = jnp.where(lane == 96, jnp.exp(-r.t1 * (LN * (KT - 1 - kf))), pick)
-            pick = jnp.where(lane == 97, jnp.exp(-r.t1 * (LN * kf)), pick)
-            high, mid, low = split3(base * pick)
-            w1[l, k] = jnp.concatenate([high, mid], axis=1)
-            w3[l, k] = low
-            return carry
-
-        lax.fori_loop(0, KT, weights, 0)
+            pick = jnp.where(lane == 96, jnp.exp(-r.t1 * jnp.full((LN, LN), float(LN * (KT - 1 - k)), F32)), pick)
+            pick = jnp.where(lane == 97, jnp.exp(-r.t1 * jnp.full((LN, LN), float(LN * k), F32)), pick)
+            for i, piece in enumerate(split3(base * pick)):
+                wt[l, k, i] = piece
+
+        for k in range(KT):
+            weights(k)
         slot = iota((32, LN), 0)
         col = fiota((32, LN), 1)
         own = (slot % 16).astype(F32)
@@ -116,19 +111,35 @@
             lt[l, L_CP, t] = scale * p
             lt[l, L_GQ, t] = scale * q * jnp.exp(-r.t2 * (local + 1.0))
             lt[l, L_GP, t] = scale * p * jnp.exp(-r.t2 * (ROWS - local))
+
+
+def move_kernel(u_hbm, m_hbm, k_hbm, ul, ml, kl, done, su, sm, sk, sem):
+    done[...] = jnp.zeros((SS, LN), F32)
+    copies = []
+    for l in range(LEV):
+        copies.append([pltpu.make_async_copy(u_hbm.at[l, :, pl.ds(k * LN, LN)], su.at[l, k], sem.at[l]) for k in range(KT)])
+    for l in range(LEV):
+        copies.append([pltpu.make_async_copy(m_hbm.at[l, :, pl.ds(k * LN, LN)], sm.at[l, k], sem.at[2 + l]) for k in range(KT)])
+    copies.append([pltpu.make_async_copy(k_hbm.at[:, pl.ds(k * LN, LN)], sk.at[k], sem.at[4]) for k in range(KT)])
     for group in copies:
         for c in group:
+            c.start()
+    for c in copies[4]:
+        c.wait()
+    for k in range(KT):
+        for t in range(TT):
+            kl[k, t] = sk[k, pl.ds(t, SS, stride=TT), :].astype(F32)
+    for l in range(LEV):
+        for c in copies[l]:
             c.wait()
-
-    def move(k, carry):
-        for t in range(TT):
-            for l in range(LEV):
+        for k in range(KT):
+            for t in range(TT):
                 ul[l, k, t] = su[l, k, pl.ds(t, SS, stride=TT), :]
+        for c in copies[2 + l]:
+            c.wait()
+        for k in range(KT):
+            for t in range(TT):
                 ml[l, k, t] = sm[l, k, pl.ds(t, SS, stride=TT), :]
-            kl[k, t] = sk[k, pl.ds(t, SS, stride=TT), :].astype(F32)
-        return carry
-
-    lax.fori_loop(0, KT, move, 0)
 
 
 def turned(tiles, ext):
@@ -186,28 +197,20 @@
     return jnp.exp(jnp.full((SS, LN), -1.0, F32) * t2)
 
 
-def local_solve(par, qs, xs, ss, w1, w3, k1, k3, et, lt, zl, phi, with_p):
+def local_solve(par, qs, xs, ss, wt, kt, et, lt, zl, phi, with_p):
     sums = []
     for l in range(LEV):
         r = Rates(par, l)
-
-        def tile(k, ab):
-            high, mid, low = split3(qs[l, k].reshape(ROWS, LN))
-            lhs1 = jnp.concatenate([high, mid], axis=1)
-            lhs2 = jnp.concatenate([low, high], axis=1)
-            kk = k1[l]
-            one = dot(lhs1, jnp.concatenate([kk, kk], axis=0))
-            two = dot(lhs2, jnp.concatenate([kk[:, :LN], k3[l]], axis=0))
-            x = (one[:, :LN] + one[:, LN:] + two).reshape(TT, SS, LN)
-            xs[l, k] = xs[l, k] + x if with_p else x
-            ww = w1[l, k]
-            one = dot(lhs1, jnp.concatenate([ww, ww], axis=0))
-            two = dot(lhs2, jnp.concatenate([ww[:, :LN], w3[l, k]], axis=0))
-            return ab + (one[:, :LN] + one[:, LN:] + two)
 
         ab = jnp.zeros((ROWS, LN), F32)
         for k in range(KT):
-            ab = tile(k, ab)
+            high, mid, low = split3(qs[l, k].reshape(ROWS, LN))
+            lhs = jnp.concatenate([high, mid, low, high, high, mid], axis=1)
+            pieces = [jnp.concatenate([kt[l, i], wt[l, k, i]], axis=1) for i in (0, 0, 0, 2, 1, 1)]
+            both = dot(lhs, jnp.concatenate(pieces, axis=0))
+            x = both[:, :LN].reshape(TT, SS, LN)
+            xs[l, k] = xs[l, k] + x if with_p else x
+            ab = ab + both[:, LN:]
         sums.append(ab)
         high, mid, low = split3(ab)
         lane = iota((ROWS, LN), 1)
@@ -268,7 +271,7 @@
     return turned[0:1], turned[LN - 1 : LN]
 
 
-def first_kernel(par, ul, ml, kl, north, south, w1, w3, k1, k3, et, lt, zl, phi, msg, uh, kh, qs, xs, ss):
+def first_kernel(par, ul, ml, kl, north, south, wt, kt, et, lt, zl, phi, msg, uh, kh, qs, xs, ss):
     def spread(ref, row):
         return jnp.stack([jnp.broadcast_to(ref[row, k : k + 1, :], (SS, LN)) for k in range(KT)])
 
@@ -289,7 +292,7 @@
             else:
                 after = lambda k, t=t: ul[l, k, t + 1]
             explicit(r, l, t, before, lambda k, t=t: ul[l, k, t], after, None, None, ml, kl, qs, xs)
-    sums = local_solve(par, qs, xs, ss, w1, w3, k1, k3, et, lt, zl, phi, True)
+    sums = local_solve(par, qs, xs, ss, wt, kt, et, lt, zl, phi, True)
     parts = []
     for l in range(LEV):
         parts.append(sums[l].T[96:98])
@@ -336,7 +339,7 @@
         par, got, phi, lt, el, out, pack, ze, ux, kx, uhx, khx = refs
     else:
         par, got, phi, px, lt, el, out, pack, ze = refs
-    i_pos, j_pos = position(par)
+    i_pos, j_pos = position()
     peer = fiota((NLON_DEV, LN), 0)
     mine = peer == j_pos
     fluxes = []
@@ -453,7 +456,7 @@
 
 
 def arrive(par, got, pack, tb, vb, hb):
-    i_pos, _ = position(par)
+    i_pos, _ = position()
     zero = jnp.zeros((PK, LN), F32)
     above, below = zero, zero
     for p in range(NLAT_DEV):
@@ -507,7 +510,7 @@
         msg[j] = block
 
 
-def half_kernel(par, got, pack, zl, ze, ul, ux, uh, uhx, ml, el, w1, w3, k1, k3, et, lt,
+def half_kernel(par, got, pack, zl, ze, ul, ux, uh, uhx, ml, el, wt, kt, et, lt,
                 y2, yx, yh, zo, phi, msg, px, tb, vb, vs, qs, xs, ss):
     arrive(par, got, pack, tb, vb, yh)
     for l in range(LEV):
@@ -531,10 +534,10 @@
             diff = [vs[k, t + 2] - vs[k, t] for k in range(KT + 1)]
             for k, (east, west) in enumerate(turned(lambda k: diff[k], diff[KT])):
                 qs[l, k, t] = 0.5 * ml[l, k, t] * (east - west)
-    send_sums(local_solve(par, qs, xs, ss, w1, w3, k1, k3, et, lt, zo, phi, False), msg)
-
-
-def step_kernel(par, got, pack, zl, ze, y2, yx, yh, kl, kx, kh, khx, ml, el, w1, w3, k1, k3, et, lt,
+    send_sums(local_solve(par, qs, xs, ss, wt, kt, et, lt, zo, phi, False), msg)
+
+
+def step_kernel(par, got, pack, zl, ze, y2, yx, yh, kl, kx, kh, khx, ml, el, wt, kt, et, lt,
                 un, unx, unh, unhx, zo, phi, msg, px, tb, vb, hb, vs, qs, xs, ss):
     arrive(par, got, pack, tb, vb, hb)
     for l in range(LEV):
@@ -564,19 +567,23 @@
             explicit(r, l, t, lambda k: vs[k, t], lambda k: vs[k, t + 1], lambda k: vs[k, t + 2],
                      here, after - before, ml, kl, qs, xs)
             px[l, t] = jnp.where(iota((SS, LN), 1) < 2, -r.a2 * (after + before - 2.0 * here), 0.0)
-    send_sums(local_solve(par, qs, xs, ss, w1, w3, k1, k3, et, lt, zo, phi, True), msg)
-
-
-def last_kernel(par, got, pack, zl, ze, y2, kl, el, lt, out, tb, vb, os, sem):
+    send_sums(local_solve(par, qs, xs, ss, wt, kt, et, lt, zo, phi, True), msg)
+
+
+def last_kernel(par, got, pack, zl, ze, y2, kl, el, lt, out, tb, vb, zs, os, sem):
     arrive(par, got, pack, tb, vb, None)
     copies = []
     for l in range(LEV):
-
-        def use(k, t, own):
-            os[l, k, pl.ds(t, SS, stride=TT), :] = kl[k, t] * (own + y2[l, k, t])
-
-        solved_rows(l, zl, ze, el, lt, tb, vb, use, None)
         for k in range(KT):
+            e_left, e_right, above, below = el[l, 0, k], el[l, 1, k], tb[l, k], vb[l, k]
+            for t in range(TT):
+                if k == 0:
+                    extra = ze[l, t]
+                    zs[0, t] = jnp.broadcast_to(extra[:, 2:3], (SS, LN))
+                    zs[1, t] = jnp.broadcast_to(extra[:, 3:4], (SS, LN))
+                z = zl[l, k, t] + e_left * zs[0, t] + e_right * zs[1, t]
+                z = z + lt[l, L_GQ, t] * above + lt[l, L_GP, t] * below
+                os[l, k, pl.ds(t, SS, stride=TT), :] = kl[k, t] * (z + y2[l, k, t])
             copies.append(pltpu.make_async_copy(os.at[l, k], out.at[l, :, pl.ds(k * LN, LN)], sem.at[l]))
             copies[-1].start()
     for c in copies:
@@ -589,14 +596,14 @@
 FLUX = (LEV, 2, KT, SS, LN)
 
 
-def call(kernel, outs, ins, scratch=(), out_specs=None, in_specs=None):
+def call(kernel, outs, ins, scratch=(), out_specs=None, in_specs=None, limit=10):
     return pl.pallas_call(
         kernel,
         out_shape=outs,
         in_specs=in_specs or [SM] + [VM] * (len(ins) - 1),
         out_specs=out_specs or [VM] * len(outs),
         scratch_shapes=list(scratch),
-        compiler_params=PARAMS,
+        compiler_params=pltpu.CompilerParams(vmem_limit_bytes=limit * 1024 * 1024),
     )(*ins)
 
 
@@ -604,26 +611,44 @@
     return pltpu.VMEM(dims, F32)
 
 
+def rows_kernel(u_hbm, k_hbm, one, two, su, sk, sem):
+    copies = []
+    for side, at in ((0, 0), (1, ROWS - SS)):
+        for l in range(LEV):
+            copies.append(pltpu.make_async_copy(u_hbm.at[l, pl.ds(at, SS)], su.at[l, side], sem.at[l, side]))
+        copies.append(pltpu.make_async_copy(k_hbm.at[pl.ds(at, SS)], sk.at[side], sem.at[LEV, side]))
+    for c in copies:
+        c.start()
+    for c in copies:
+        c.wait()
+    even = jnp.full((1, LN), lax.axis_index("lat") % 2, jnp.int32) == 0
+    for k in range(KT):
+        at = pl.ds(k * LN, LN)
+        for row in range(LEV + 1):
+            if row < LEV:
+                first, last = su[row, 0, 0:1, at], su[row, 1, SS - 1 : SS, at]
+            else:
+                first, last = sk[0, 0:1, at].astype(F32), sk[1, SS - 1 : SS, at].astype(F32)
+            one[row, k : k + 1, :] = jnp.where(even, last, first)
+            two[row, k : k + 1, :] = jnp.where(even, first, last)
+
+
 def halo_rows(ensemble, mask):
-    at = lax.axis_index("lat")
-    first = jnp.concatenate([ensemble[:, 0, 0, :], mask[0:1, :].astype(F32)], axis=0).reshape(3, KT, LN)
-    last = jnp.concatenate([ensemble[:, 0, ROWS - 1, :], mask[ROWS - 1 :, :].astype(F32)], axis=0).reshape(3, KT, LN)
-    even = at % 2 == 0
+    one, two = call(
+        rows_kernel,
+        [shape(LEV + 1, KT, LN), shape(LEV + 1, KT, LN)],
+        [ensemble[:, 0], mask],
+        [vmem(LEV, 2, SS, COLS), pltpu.VMEM((2, SS, COLS), jnp.int32), pltpu.SemaphoreType.DMA((LEV + 1, 2))],
+        in_specs=[HB, HB],
+        limit=57,
+    )
     pairs = [(i, i + 1) for i in range(0, NLAT_DEV, 2)]
     odd_pairs = [(i, i + 1) for i in range(1, NLAT_DEV - 1, 2)]
     both = lambda edges: edges + [(j, i) for i, j in edges]
-    one = lax.ppermute(jnp.where(even, last, first), "lat", both(pairs))
-    two = lax.ppermute(jnp.where(even, first, last), "lat", both(odd_pairs))
+    one = lax.ppermute(one, "lat", both(pairs))
+    two = lax.ppermute(two, "lat", both(odd_pairs))
+    even = lax.axis_index("lat") % 2 == 0
     return jnp.where(even, two, one), jnp.where(even, one, two)
-
-
-def parameters(level_rates):
-    a = level_rates
-    half = 0.5 / jnp.sqrt(a)
-    theta = 2.0 * jnp.log1p(half + half * half / (1.0 + jnp.sqrt(1.0 + half * half)))
-    scale = 1.0 / jnp.sqrt(1.0 + 4.0 * a)
-    where = jnp.stack([lax.axis_index("lat"), lax.axis_index("lon")]).astype(F32)
-    return jnp.concatenate([jnp.stack([theta, a, scale]).reshape(-1), where])
 
 
 def exchange(values, axis):
@@ -631,23 +656,27 @@
 
 
 def shards(ensemble, cross_mix, sea_mask, level_rates, panel_inverse, reduced_lon, reduced_lat):
-    par = parameters(level_rates)
+    par = level_rates
     north, south = halo_rows(ensemble, sea_mask)
     work = [vmem(*FIELD), vmem(*FIELD), vmem(KT, TT, SS, LN)]
     carries = [vmem(LEV, KT + 1, SS, LN), vmem(LEV, KT + 1, SS, LN)]
     diffs = vmem(KT + 1, TT + 2, SS, LN)
-    ul, ml, kl, w1, w3, k1, k3, et, lt, el = call(
-        tables_kernel,
-        [shape(*FIELD), shape(*FIELD), shape(KT, TT, SS, LN),
-         shape(LEV, KT, LN, 2 * LN, dtype=BF16), shape(LEV, KT, LN, LN, dtype=BF16),
-         shape(LEV, LN, 2 * LN, dtype=BF16), shape(LEV, LN, LN, dtype=BF16),
-         shape(LEV, 2 * LN, COLS, dtype=BF16), shape(LEV, 8, TT, SS, LN), shape(LEV, 2, KT, SS, LN)],
-        [par, ensemble[:, 0], cross_mix, sea_mask],
+    ul, ml, kl, done = call(
+        move_kernel,
+        [shape(*FIELD), shape(*FIELD), shape(KT, TT, SS, LN), shape(SS, LN)],
+        [ensemble[:, 0], cross_mix, sea_mask],
         [vmem(LEV, KT, ROWS, LN), vmem(LEV, KT, ROWS, LN), pltpu.VMEM((KT, ROWS, LN), jnp.int32),
          pltpu.SemaphoreType.DMA((5,))],
-        in_specs=[SM, HB, HB, HB],
+        in_specs=[HB, HB, HB],
+        limit=45,
     )
-    mats = [w1, w3, k1, k3, et, lt]
+    wt, kt, et, lt, el = call(
+        tables_kernel,
+        [shape(LEV, KT, 3, LN, LN, dtype=BF16), shape(LEV, 3, LN, LN, dtype=BF16),
+         shape(LEV, 2 * LN, COLS, dtype=BF16), shape(LEV, 8, TT, SS, LN), shape(LEV, 2, KT, SS, LN)],
+        [par, done],
+    )
+    mats = [wt, kt, et, lt]
     solve_out = [shape(*FIELD), shape(*FLUX), shape(NLON_DEV, 8, LN)]
     carry_out = [shape(NLAT_DEV, PK, LN), shape(2, PK, LN), shape(*EXTRA)]
     zl, phi, msg, uh, kh = call(
@@ -687,7 +716,7 @@
         last_kernel,
         [shape(LEV, ROWS, COLS)],
         [par, got, pack, zl, ze, y2, kl, el, lt],
-        carries + [vmem(LEV, KT, ROWS, LN), pltpu.SemaphoreType.DMA((LEV,))],
+        carries + [vmem(2, TT, SS, LN), vmem(LEV, KT, ROWS, LN), pltpu.SemaphoreType.DMA((LEV,))],
         out_specs=[HB],
     )
     return final[:, None]

time: 145 us -> 133 us (0.917)
  local copies, waits for them, and re-layouts: 5.49 us -> 0.01 us
  Pallas kernels: 38.6 us -> 35.3 us
  other arithmetic: 2.46 us -> 0.01 us
    unnamed x6, local copies, waits for them, and re-layouts: 4.41 us -> 0.01 us
    pallas_call x10 -> x12, Pallas kernels: 38.6 us -> 35.3 us  [call(): pl.pallas_call(kernel, out_shape=outs, in_specs=in_specs or [SM] + [VM] *...]
  transfers between devices with their start and end apart: 2 -> 2, of which waited for: 0 -> 0; matrix products, arithmetic and copies ran while one was open for 1% -> 0% of each run, Pallas kernels for 4% -> 3%
where the time goes in v3:
time: 133 us
  blocking collectives  92.4 us (69%)
  Pallas kernels  35.3 us (27%)
  starting transfers between devices  4.59 us (3%)
    all_to_all x8, blocking collectives, exchange(): return lax.all_to_all(values, axis, split_axis=0, concat_axis=0, tiled=True)  92.4 us
    pallas_call x12, Pallas kernels, call(): pl.pallas_call(kernel, out_shape=outs, in_specs=in_specs or [SM] + [VM] *...  35.3 us
    ppermute x1, starting transfers between devices, halo_rows(): two = lax.ppermute(two, 'lat', both(odd_pairs))  4.51 us
  transfers between devices with their start and end apart: 2, of which 0 were waited for; matrix products, arithmetic and copies ran while one was open for 0% of the time, Pallas kernels for 3%

profile of v3, /device:TPU:1, one launch (start us, length us, event | category | flops | bytes accessed | tf_op | source)
XLA Modules:
  0.0 132.7 jit_solution(8774021671794822402)
XLA Ops:
  0.0 1.8 %shard_map.47 = (f32[3,16,128]{2,1,0:T(8,128)}, f32[3,16,128]{2,1,0:T(8,128)}) custom-call(f32[2,128,2048]{2,1,0:T(8,128)} %bitcast.4, s32[128,2048]{1,0:T(8,128)} %k_hbm.3), custom_call_target="tpu_custom_call" | custom-call | tf_op jit(solution)/shard_map/pallas_call | solution.py:600
  1.9 4.5 %collective-permute-start = (f32[3,16,128]{2,1,0:T(8,128)}, f32[3,16,128]{2,1,0:T(8,128)S(1)}, u32[]{:S(2)}, u32[]{:S(2)}) collective-permute-start(f32[3,16,128]{2,1,0:T(8,128)} %get-tuple-element.60), channel_id=1, source_target_pairs={{8,16},{24,32},{40,48},{56,64},{72,80},{88,96},{104,112},{16,8},{3... | collective-permute-start | bytes 73736 | tf_op jit(solution)/shard_map/ppermute | solution.py:649
  6.4 0.1 collective-permute-start.1
  6.5 0.0 copy-start.2
  6.5 2.6 %shard_map.46 = (f32[2,16,16,8,128]{4,3,2,1,0:T(8,128)S(1)}, f32[2,16,16,8,128]{4,3,2,1,0:T(8,128)S(1)}, f32[16,16,8,128]{3,2,1,0:T(8,128)S(1)}, f32[8,128]{1,0:T(8,128)S(1)}) custom-call(f32[2,128,2048]{2,1,0:T(8,128)S(1)} %bitcast.5, f32[2,128,2048]{2,1,0:T(8,128)} %m_hbm.1, s32[128,2048]{1,0:T(8,128)S(1)} %copy-done.1), custom_call_target="tpu_custom_call" | custom-call | tf_op jit(solution)/shard_map/pallas_call | solution.py:600
  9.2 1.8 %shard_map.48 = (bf16[2,16,3,128,128]{4,3,2,1,0:T(8,128)(2,1)S(1)}, bf16[2,3,128,128]{3,2,1,0:T(8,128)(2,1)S(1)}, bf16[2,256,2048]{2,1,0:T(8,128)(2,1)S(1)}, f32...) custom-call(f32[2,2]{1,0:T(2,128)S(1)} %copy-done.2, f32[8,128]{1,0:T(8,128)S(1)} %get-tuple-element.62.after), custom_call_target="tpu_custom_call" | custom-call | tf_op jit(solution)/shard_map/pallas_call | solution.py:600
  11.0 0.0 collective-permute-done
  11.0 5.3 %shard_map.49 = (f32[2,16,16,8,128]{4,3,2,1,0:T(8,128)S(1)}, f32[2,2,16,8,128]{4,3,2,1,0:T(8,128)S(1)}, f32[8,24,128]{2,1,0:T(8,128)S(1)}, f32[2,2,17,8,128]{4,3,2,1,0:T(8,128)S(1)}, f32[2,17,8,128]{3,2,1,0:T(8,128)S(1)}) custom-call(f32[2,2]{1,0:T(2,128)S(1)} %copy-done.2, f32[2,16,16,8,128]{4,3,2,1,0:T(8,128)S(1)} %get-tuple-element.57.ul, ...), custom_call_target="tpu_custom_call" | custom-call | tf_op jit(solution)/shard_map/pallas_call | solution.py:600
  16.4 11.1 %all_to_all.40.refs_1_ = f32[8,24,128]{2,1,0:T(8,128)S(1)} all-to-all(f32[8,24,128]{2,1,0:T(8,128)S(1)} %get-tuple-element.67), channel_id=1, replica_groups=mesh['lat'=16,'lon'=8] {'lon'}, dimensions={0} | all-to-all | bytes 196608 | tf_op jit(solution)/shard_map/all_to_all | solution.py:655
  27.5 1.0 shard_map.50
  28.6 17.1 %all_to_all.41.got = f32[16,40,128]{2,1,0:T(8,128)S(1)} all-to-all(f32[16,40,128]{2,1,0:T(8,128)S(1)} %get-tuple-element.70), channel_id=1, replica_groups=mesh['lat'=16,'lon'=8] {'lat'}, dimensions={0} | all-to-all | bytes 655360 | tf_op jit(solution)/shard_map/all_to_all | solution.py:655
  45.7 5.2 %shard_map.51 = (f32[2,16,16,8,128]{4,3,2,1,0:T(8,128)S(1)}, f32[2,16,8,128]{3,2,1,0:T(8,128)S(1)}, f32[2,2,17,8,128]{4,3,2,1,0:T(8,128)S(1)}, f32[2,16,16,8,128...) custom-call(f32[2,2]{1,0:T(2,128)S(1)} %copy-done.2, ...), custom_call_target="tpu_custom_call" | custom-call | tf_op jit(solution)/shard_map/pallas_call | solution.py:600
  50.9 7.5 %all_to_all.42.refs_1_ = f32[8,8,128]{2,1,0:T(8,128)S(1)} all-to-all(f32[8,8,128]{2,1,0:T(8,128)S(1)} %get-tuple-element.77), channel_id=1, replica_groups=mesh['lat'=16,'lon'=8] {'lon'}, dimensions={0} | all-to-all | bytes 65536 | tf_op jit(solution)/shard_map/all_to_all | solution.py:655
  58.3 0.9 shard_map.52
  59.3 13.8 %all_to_all.43.got = f32[16,40,128]{2,1,0:T(8,128)S(1)} all-to-all(f32[16,40,128]{2,1,0:T(8,128)S(1)} %get-tuple-element.80), channel_id=1, replica_groups=mesh['lat'=16,'lon'=8] {'lat'}, dimensions={0} | all-to-all | bytes 655360 | tf_op jit(solution)/shard_map/all_to_all | solution.py:655
  73.1 6.5 %shard_map.53 = (f32[2,16,16,8,128]{4,3,2,1,0:T(8,128)S(1)}, f32[2,16,8,128]{3,2,1,0:T(8,128)S(1)}, f32[2,2,17,8,128]{4,3,2,1,0:T(8,128)S(1)}, f32[2,2,8,128]{3,...) custom-call(f32[2,2]{1,0:T(2,128)S(1)} %copy-done.2, ...), custom_call_target="tpu_custom_call" | custom-call | tf_op jit(solution)/shard_map/pallas_call | solution.py:600
  79.6 7.5 %all_to_all.44.refs_1_ = f32[8,8,128]{2,1,0:T(8,128)S(1)} all-to-all(f32[8,8,128]{2,1,0:T(8,128)S(1)} %get-tuple-element.90), channel_id=1, replica_groups=mesh['lat'=16,'lon'=8] {'lon'}, dimensions={0} | all-to-all | bytes 65536 | tf_op jit(solution)/shard_map/all_to_all | solution.py:655
  87.1 0.9 shard_map.54
  88.1 14.1 %all_to_all.45.got = f32[16,40,128]{2,1,0:T(8,128)S(1)} all-to-all(f32[16,40,128]{2,1,0:T(8,128)S(1)} %get-tuple-element.93), channel_id=1, replica_groups=mesh['lat'=16,'lon'=8] {'lat'}, dimensions={0} | all-to-all | bytes 655360 | tf_op jit(solution)/shard_map/all_to_all | solution.py:655
  102.2 5.2 %shard_map.55 = (f32[2,16,16,8,128]{4,3,2,1,0:T(8,128)S(1)}, f32[2,16,8,128]{3,2,1,0:T(8,128)}, f32[2,2,17,8,128]{4,3,2,1,0:T(8,128)}, f32[2,16,16,8,128]{4,3,2,...) custom-call(f32[2,2]{1,0:T(2,128)S(1)} %copy-done.2, ...), custom_call_target="tpu_custom_call" | custom-call | tf_op jit(solution)/shard_map/pallas_call | solution.py:600
  107.3 7.5 %all_to_all.46.refs_1_ = f32[8,8,128]{2,1,0:T(8,128)S(1)} all-to-all(f32[8,8,128]{2,1,0:T(8,128)S(1)} %get-tuple-element.101), channel_id=1, replica_groups=mesh['lat'=16,'lon'=8] {'lon'}, dimensions={0} | all-to-all | bytes 65536 | tf_op jit(solution)/shard_map/all_to_all | solution.py:655
  114.8 0.9 shard_map.56
  115.8 13.8 %all_to_all.47.got = f32[16,40,128]{2,1,0:T(8,128)S(1)} all-to-all(f32[16,40,128]{2,1,0:T(8,128)S(1)} %get-tuple-element.104), channel_id=1, replica_groups=mesh['lat'=16,'lon'=8] {'lat'}, dimensions={0} | all-to-all | bytes 655360 | tf_op jit(solution)/shard_map/all_to_all | solution.py:655
  129.6 2.9 %shard_map.57 = f32[2,128,2048]{2,1,0:T(8,128)} custom-call(f32[2,2]{1,0:T(2,128)S(1)} %copy-done.2, f32[16,40,128]{2,1,0:T(8,128)S(1)} %all_to_all.47.got, f32[2,40,128]{2,1,0:T(8,128)S(1)} %get-tuple-element.105.pack, f32[2,16,16,8,128]{4,3,2,1,0:T(8,128)S(1)} %get-tuple-element.106.zl, f32[2,16,8,128]{3,2,1,0:T(8,128)S(1)} %get-tuple-element.107.ze, ...), custom_call_target="tpu_custom_call" | custom-call | tf_op jit(solution)/shard_map/pallas_call | solution.py:600
  (7 shorter events, 0.0 us)
Async XLA Ops:
  0.0 6.5 %copy-start.1 = (s32[128,2048]{1,0:T(8,128)S(1)}, s32[128,2048]{1,0:T(8,128)}, u32[]{:S(2)}) copy-start(s32[128,2048]{1,0:T(8,128)} %k_hbm.3) | copy-start | bytes 3145732
  0.0 6.5 %copy-start = (f32[2,1,128,2048]{3,2,1,0:T(8,128)S(1)}, f32[2,1,128,2048]{3,2,1,0:T(8,128)}, u32[]{:S(2)}) copy-start(f32[2,1,128,2048]{3,2,1,0:T(8,128)} %param.7) | copy-start | bytes 6291460
  1.9 9.1 %collective-permute-start = (f32[3,16,128]{2,1,0:T(8,128)}, f32[3,16,128]{2,1,0:T(8,128)S(1)}, u32[]{:S(2)}, u32[]{:S(2)}) collective-permute-start(f32[3,16,128]{2,1,0:T(8,128)} %get-tuple-element.60), channel_id=1, source_target_pairs={{8,16},{24,32},{40,48},{56,64},{72,80},{88,96},{104,112},{16,8},{3... | collective-permute-start | bytes 73736 | tf_op jit(solution)/shard_map/ppermute | solution.py:649
  6.4 4.6 %collective-permute-start.1 = (f32[3,16,128]{2,1,0:T(8,128)}, f32[3,16,128]{2,1,0:T(8,128)S(1)}, u32[]{:S(2)}, u32[]{:S(2)}) collective-permute-start(f32[3,16,128]{2,1,0:T(8,128)} %get-tuple-element.61), channel_id=1, source_target_pairs={{0,8},{16,24},{32,40},{48,56},{64,72},{80,88},{96,104},{112,120},{... | collective-permute-start | bytes 73736 | tf_op jit(solution)/shard_map/ppermute | solution.py:648
  6.5 2.7 %copy-start.2 = (f32[2,2]{1,0:T(2,128)S(1)}, f32[2,2]{1,0:T(2,128)}, u32[]{:S(2)}) copy-start(f32[2,2]{1,0:T(2,128)} %par.11) | copy-start | bytes 52

commit v4 on v3

--- a/solution.py
+++ b/solution.py
@@ -216,36 +216,23 @@
         lane = iota((ROWS, LN), 1)
         second = jnp.where(lane < 64, mid.astype(F32), low.astype(F32)).astype(BF16)
         lhs = jnp.concatenate([high, second], axis=1)
-        for k in range(0, KT, 2):
-            fix = dot(lhs, et[l, :, pl.ds(k * LN, 2 * LN)])
-            xs[l, k] += fix[:, :LN].reshape(TT, SS, LN)
-            xs[l, k + 1] += fix[:, LN:].reshape(TT, SS, LN)
-
         lam = lam2(r.t2)
-
-        def down(t, carry):
-            s, acc = carry
-            x = xs[l, :, t]
-            s = lam * s + lt[l, L_P, t] * x
-            ss[:, t] = s
-            return s, acc + lt[l, L_LQ, t] * x
-
-        zero = jnp.zeros((KT, SS, LN), F32)
-        last, acc = zero, zero
-        for t in range(TT):
-            last, acc = down(t, (last, acc))
-        carry_down, carry_up, phi_l, psi_l = chunk_ends(last, acc, r.t2)
-        phi[l, 0] = phi_l
-        phi[l, 1] = psi_l
-
-        def up(i, u):
-            t = TT - 1 - i
-            zl[l, :, t] = lt[l, L_CQ, t] * ss[:, t] + lt[l, L_CQL, t] * carry_down + lt[l, L_CP, t] * u
-            return lam * (u + lt[l, L_Q, t] * xs[l, :, t])
-
-        u = lam * carry_up
-        for i in range(TT):
-            u = up(i, u)
+        zero = jnp.zeros((SS, LN), F32)
+        for pair in range(0, KT, 2):
+            fix = dot(lhs, et[l, :, pl.ds(pair * LN, 2 * LN)])
+            for k in (pair, pair + 1):
+                at = (k - pair) * LN
+                x = xs[l, k] + fix[:, at : at + LN].reshape(TT, SS, LN)
+                last, acc, kept = zero, zero, []
+                for t in range(TT):
+                    last = lam * last + lt[l, L_P, t] * x[t]
+                    acc = acc + lt[l, L_LQ, t] * x[t]
+                    kept.append(last)
+                carry_down, carry_up, phi[l, 0, k], phi[l, 1, k] = chunk_ends(last, acc, r.t2)
+                u = lam * carry_up
+                for t in range(TT - 1, -1, -1):
+                    zl[l, k, t] = lt[l, L_CQ, t] * kept[t] + lt[l, L_CQL, t] * carry_down + lt[l, L_CP, t] * u
+                    u = lam * (u + lt[l, L_Q, t] * x[t])
     return sums
 
 

time: 133 us -> 133 us (level)
  no operation moved by 1% of the time
where the time goes in v4:
time: 133 us
  blocking collectives  92.4 us (69%)
  Pallas kernels  35.3 us (27%)
  starting transfers between devices  4.59 us (3%)
    all_to_all x8, blocking collectives, exchange(): return lax.all_to_all(values, axis, split_axis=0, concat_axis=0, tiled=True)  92.4 us
    pallas_call x12, Pallas kernels, call(): pl.pallas_call(kernel, out_shape=outs, in_specs=in_specs or [SM] + [VM] *...  35.3 us
    ppermute x1, starting transfers between devices, halo_rows(): two = lax.ppermute(two, 'lat', both(odd_pairs))  4.51 us
  transfers between devices with their start and end apart: 2, of which 0 were waited for; matrix products, arithmetic and copies ran while one was open for 0% of the time, Pallas kernels for 3%

profile of v4, /device:TPU:1, one launch (start us, length us, event | category | flops | bytes accessed | tf_op | source)
XLA Modules:
  0.0 132.7 jit_solution(14321629565446243332)
XLA Ops:
  0.0 1.8 %shard_map.47 = (f32[3,16,128]{2,1,0:T(8,128)}, f32[3,16,128]{2,1,0:T(8,128)}) custom-call(f32[2,128,2048]{2,1,0:T(8,128)} %bitcast.4, s32[128,2048]{1,0:T(8,128)} %k_hbm.3), custom_call_target="tpu_custom_call" | custom-call | tf_op jit(solution)/shard_map/pallas_call | solution.py:587
  1.9 4.5 %collective-permute-start = (f32[3,16,128]{2,1,0:T(8,128)}, f32[3,16,128]{2,1,0:T(8,128)S(1)}, u32[]{:S(2)}, u32[]{:S(2)}) collective-permute-start(f32[3,16,128]{2,1,0:T(8,128)} %get-tuple-element.60), channel_id=1, source_target_pairs={{8,16},{24,32},{40,48},{56,64},{72,80},{88,96},{104,112},{16,8},{3... | collective-permute-start | bytes 73736 | tf_op jit(solution)/shard_map/ppermute | solution.py:636
  6.4 0.1 collective-permute-start.1
  6.5 0.0 copy-start.2
  6.5 2.6 %shard_map.46 = (f32[2,16,16,8,128]{4,3,2,1,0:T(8,128)S(1)}, f32[2,16,16,8,128]{4,3,2,1,0:T(8,128)S(1)}, f32[16,16,8,128]{3,2,1,0:T(8,128)S(1)}, f32[8,128]{1,0:T(8,128)S(1)}) custom-call(f32[2,128,2048]{2,1,0:T(8,128)S(1)} %bitcast.5, f32[2,128,2048]{2,1,0:T(8,128)} %m_hbm.1, s32[128,2048]{1,0:T(8,128)S(1)} %copy-done.1), custom_call_target="tpu_custom_call" | custom-call | tf_op jit(solution)/shard_map/pallas_call | solution.py:587
  9.2 1.8 %shard_map.48 = (bf16[2,16,3,128,128]{4,3,2,1,0:T(8,128)(2,1)S(1)}, bf16[2,3,128,128]{3,2,1,0:T(8,128)(2,1)S(1)}, bf16[2,256,2048]{2,1,0:T(8,128)(2,1)S(1)}, f32...) custom-call(f32[2,2]{1,0:T(2,128)S(1)} %copy-done.2, f32[8,128]{1,0:T(8,128)S(1)} %get-tuple-element.62.after), custom_call_target="tpu_custom_call" | custom-call | tf_op jit(solution)/shard_map/pallas_call | solution.py:587
  11.0 0.0 collective-permute-done
  11.0 5.4 %shard_map.49 = (f32[2,16,16,8,128]{4,3,2,1,0:T(8,128)S(1)}, f32[2,2,16,8,128]{4,3,2,1,0:T(8,128)S(1)}, f32[8,24,128]{2,1,0:T(8,128)S(1)}, f32[2,2,17,8,128]{4,3,2,1,0:T(8,128)S(1)}, f32[2,17,8,128]{3,2,1,0:T(8,128)S(1)}) custom-call(f32[2,2]{1,0:T(2,128)S(1)} %copy-done.2, f32[2,16,16,8,128]{4,3,2,1,0:T(8,128)S(1)} %get-tuple-element.57.ul, ...), custom_call_target="tpu_custom_call" | custom-call | tf_op jit(solution)/shard_map/pallas_call | solution.py:587
  16.4 11.1 %all_to_all.40.refs_1_ = f32[8,24,128]{2,1,0:T(8,128)S(1)} all-to-all(f32[8,24,128]{2,1,0:T(8,128)S(1)} %get-tuple-element.67), channel_id=1, replica_groups=mesh['lat'=16,'lon'=8] {'lon'}, dimensions={0} | all-to-all | bytes 196608 | tf_op jit(solution)/shard_map/all_to_all | solution.py:642
  27.5 1.0 shard_map.50
  28.6 17.1 %all_to_all.41.got = f32[16,40,128]{2,1,0:T(8,128)S(1)} all-to-all(f32[16,40,128]{2,1,0:T(8,128)S(1)} %get-tuple-element.70), channel_id=1, replica_groups=mesh['lat'=16,'lon'=8] {'lat'}, dimensions={0} | all-to-all | bytes 655360 | tf_op jit(solution)/shard_map/all_to_all | solution.py:642
  45.7 5.2 %shard_map.51 = (f32[2,16,16,8,128]{4,3,2,1,0:T(8,128)S(1)}, f32[2,16,8,128]{3,2,1,0:T(8,128)S(1)}, f32[2,2,17,8,128]{4,3,2,1,0:T(8,128)S(1)}, f32[2,16,16,8,128...) custom-call(f32[2,2]{1,0:T(2,128)S(1)} %copy-done.2, ...), custom_call_target="tpu_custom_call" | custom-call | tf_op jit(solution)/shard_map/pallas_call | solution.py:587
  50.9 7.5 %all_to_all.42.refs_1_ = f32[8,8,128]{2,1,0:T(8,128)S(1)} all-to-all(f32[8,8,128]{2,1,0:T(8,128)S(1)} %get-tuple-element.77), channel_id=1, replica_groups=mesh['lat'=16,'lon'=8] {'lon'}, dimensions={0} | all-to-all | bytes 65536 | tf_op jit(solution)/shard_map/all_to_all | solution.py:642
  58.4 0.9 shard_map.52
  59.3 13.8 %all_to_all.43.got = f32[16,40,128]{2,1,0:T(8,128)S(1)} all-to-all(f32[16,40,128]{2,1,0:T(8,128)S(1)} %get-tuple-element.80), channel_id=1, replica_groups=mesh['lat'=16,'lon'=8] {'lat'}, dimensions={0} | all-to-all | bytes 655360 | tf_op jit(solution)/shard_map/all_to_all | solution.py:642
  73.1 6.5 %shard_map.53 = (f32[2,16,16,8,128]{4,3,2,1,0:T(8,128)S(1)}, f32[2,16,8,128]{3,2,1,0:T(8,128)S(1)}, f32[2,2,17,8,128]{4,3,2,1,0:T(8,128)S(1)}, f32[2,2,8,128]{3,...) custom-call(f32[2,2]{1,0:T(2,128)S(1)} %copy-done.2, ...), custom_call_target="tpu_custom_call" | custom-call | tf_op jit(solution)/shard_map/pallas_call | solution.py:587
  79.7 7.5 %all_to_all.44.refs_1_ = f32[8,8,128]{2,1,0:T(8,128)S(1)} all-to-all(f32[8,8,128]{2,1,0:T(8,128)S(1)} %get-tuple-element.90), channel_id=1, replica_groups=mesh['lat'=16,'lon'=8] {'lon'}, dimensions={0} | all-to-all | bytes 65536 | tf_op jit(solution)/shard_map/all_to_all | solution.py:642
  87.1 0.9 shard_map.54
  88.1 14.1 %all_to_all.45.got = f32[16,40,128]{2,1,0:T(8,128)S(1)} all-to-all(f32[16,40,128]{2,1,0:T(8,128)S(1)} %get-tuple-element.93), channel_id=1, replica_groups=mesh['lat'=16,'lon'=8] {'lat'}, dimensions={0} | all-to-all | bytes 655360 | tf_op jit(solution)/shard_map/all_to_all | solution.py:642
  102.2 5.2 %shard_map.55 = (f32[2,16,16,8,128]{4,3,2,1,0:T(8,128)S(1)}, f32[2,16,8,128]{3,2,1,0:T(8,128)}, f32[2,2,17,8,128]{4,3,2,1,0:T(8,128)}, f32[2,16,16,8,128]{4,3,2,...) custom-call(f32[2,2]{1,0:T(2,128)S(1)} %copy-done.2, ...), custom_call_target="tpu_custom_call" | custom-call | tf_op jit(solution)/shard_map/pallas_call | solution.py:587
  107.4 7.5 %all_to_all.46.refs_1_ = f32[8,8,128]{2,1,0:T(8,128)S(1)} all-to-all(f32[8,8,128]{2,1,0:T(8,128)S(1)} %get-tuple-element.101), channel_id=1, replica_groups=mesh['lat'=16,'lon'=8] {'lon'}, dimensions={0} | all-to-all | bytes 65536 | tf_op jit(solution)/shard_map/all_to_all | solution.py:642
  114.9 0.9 shard_map.56
  115.8 13.8 %all_to_all.47.got = f32[16,40,128]{2,1,0:T(8,128)S(1)} all-to-all(f32[16,40,128]{2,1,0:T(8,128)S(1)} %get-tuple-element.104), channel_id=1, replica_groups=mesh['lat'=16,'lon'=8] {'lat'}, dimensions={0} | all-to-all | bytes 655360 | tf_op jit(solution)/shard_map/all_to_all | solution.py:642
  129.6 2.9 %shard_map.57 = f32[2,128,2048]{2,1,0:T(8,128)} custom-call(f32[2,2]{1,0:T(2,128)S(1)} %copy-done.2, f32[16,40,128]{2,1,0:T(8,128)S(1)} %all_to_all.47.got, f32[2,40,128]{2,1,0:T(8,128)S(1)} %get-tuple-element.105.pack, f32[2,16,16,8,128]{4,3,2,1,0:T(8,128)S(1)} %get-tuple-element.106.zl, f32[2,16,8,128]{3,2,1,0:T(8,128)S(1)} %get-tuple-element.107.ze, ...), custom_call_target="tpu_custom_call" | custom-call | tf_op jit(solution)/shard_map/pallas_call | solution.py:587
  (7 shorter events, 0.0 us)
Async XLA Ops:
  0.0 6.5 %copy-start.1 = (s32[128,2048]{1,0:T(8,128)S(1)}, s32[128,2048]{1,0:T(8,128)}, u32[]{:S(2)}) copy-start(s32[128,2048]{1,0:T(8,128)} %k_hbm.3) | copy-start | bytes 3145732
  0.0 6.5 %copy-start = (f32[2,1,128,2048]{3,2,1,0:T(8,128)S(1)}, f32[2,1,128,2048]{3,2,1,0:T(8,128)}, u32[]{:S(2)}) copy-start(f32[2,1,128,2048]{3,2,1,0:T(8,128)} %param.7) | copy-start | bytes 6291460
  1.9 9.1 %collective-permute-start = (f32[3,16,128]{2,1,0:T(8,128)}, f32[3,16,128]{2,1,0:T(8,128)S(1)}, u32[]{:S(2)}, u32[]{:S(2)}) collective-permute-start(f32[3,16,128]{2,1,0:T(8,128)} %get-tuple-element.60), channel_id=1, source_target_pairs={{8,16},{24,32},{40,48},{56,64},{72,80},{88,96},{104,112},{16,8},{3... | collective-permute-start | bytes 73736 | tf_op jit(solution)/shard_map/ppermute | solution.py:636
  6.4 4.6 %collective-permute-start.1 = (f32[3,16,128]{2,1,0:T(8,128)}, f32[3,16,128]{2,1,0:T(8,128)S(1)}, u32[]{:S(2)}, u32[]{:S(2)}) collective-permute-start(f32[3,16,128]{2,1,0:T(8,128)} %get-tuple-element.61), channel_id=1, source_target_pairs={{0,8},{16,24},{32,40},{48,56},{64,72},{80,88},{96,104},{112,120},{... | collective-permute-start | bytes 73736 | tf_op jit(solution)/shard_map/ppermute | solution.py:635
  6.5 2.7 %copy-start.2 = (f32[2,2]{1,0:T(2,128)S(1)}, f32[2,2]{1,0:T(2,128)}, u32[]{:S(2)}) copy-start(f32[2,2]{1,0:T(2,128)} %par.11) | copy-start | bytes 52
